TPU v7x, 32 devices: a whole 2x2x4 slice. The times are simulated.
32 devices in a mesh: tile: 8 (over y, x, core), depth: 4 (over z).
Axes of the slice: x: 2, y: 2, z: 4, core: 2. Of those that a mesh axis runs over, the one named last changes fastest.
Arguments:
- grid: float32 [4, 32, 32, 1024], P(None, 'tile', 'depth'), may hold values from -6 to 6
- first_moment: float32 [4, 32, 32, 1024], P(None, 'tile', 'depth'), may hold values from -4 to 4
- second_moment: float32 [4, 32, 32, 1024], P(None, 'tile', 'depth'), may hold values from 0.01 to 1
- ray_offset: int32 [32, 1024], P('tile'), may hold values from 0 to 1
- occupancy: int32 [8, 4, 128], P('tile', 'depth'), may hold values 0 or 1
- target: float32 [3, 32, 1024], P(None, 'tile'), may hold values from 0 to 1
Outputs:
- new_grid: float32 [4, 32, 32, 1024], P(None, 'tile', 'depth')
- new_first: float32 [4, 32, 32, 1024], P(None, 'tile', 'depth')
- new_second: float32 [4, 32, 32, 1024], P(None, 'tile', 'depth')
All inputs are finite; a program needn't handle non-finite values. No bound on the sum of `occupancy` on one device may be relied on, other than what follows from the above.
Results may differ from a plain program's by a relative error of at most 0.00002.
Values sent between devices are 32-bit elements; how exact they have to be, the bound alone decides.
A program may use at most 64 MiB of HBM per device.

v0:
```python
import jax
import jax.numpy as jnp
from jax import lax
from jax.sharding import PartitionSpec as P

tv_weight = 0.01
beta_one = 0.9
beta_two = 0.95
learn_rate = 0.1
adam_step = 10
epsilon = 1e-08


def carried_in_2(value, axis, join, neutral, backward):
    count, mine = (lax.axis_size(axis), lax.axis_index(axis))
    pieces = jax.tree.map(lambda part: lax.all_gather(part, axis), value)
    if backward:
        pieces = jax.tree.map(lambda part: part[::-1], pieces)
        mine = count - 1 - mine
    total = jax.tree.map(
        lambda part, zero: jnp.full_like(part, 0) + jnp.asarray(zero, part.dtype), value, neutral
    )

    def lap(position, total):
        longer = join(total, jax.tree.map(lambda part: part[position], pieces))
        return jax.tree.map(lambda new, old: jnp.where(position < mine, new, old), longer, total)

    return lax.fori_loop(0, count - 1, lap, total)


def with_halo(cells, sides, width):
    for axis, dim in sides:
        count = lax.axis_size(axis)
        ends = count - 1
        head = lax.slice_in_dim(cells, 0, width, axis=dim)
        tail = lax.slice_in_dim(cells, cells.shape[dim] - width, cells.shape[dim], axis=dim)
        cells = jnp.concatenate(
            [
                lax.ppermute(tail, axis, [(i, (i + 1) % count) for i in range(ends)]),
                cells,
                lax.ppermute(head, axis, [((i + 1) % count, i) for i in range(ends)]),
            ],
            axis=dim,
        )
    return cells


def passed_along(block, axis, distance):
    devices = range(lax.axis_size(axis))
    route = [(i - distance, i) for i in devices if i - distance in devices]
    return lax.ppermute(block, axis, route)


def front_combine(earlier, later):
    return (earlier[0] + earlier[1][None] * later[0], earlier[1] * later[1])


def back_combine(earlier, later):
    return (later[0] + later[1][None] * earlier[0], later[1] * earlier[1])


def render(rows, after_rows, shares, occ, target, total_depth):
    scale = 4.0 / total_depth
    features = (1.0 - shares) * rows + shares * after_rows
    sigma = occ * jax.nn.softplus(features[0]) * scale
    colour = jax.nn.sigmoid(features[1:])
    before = jnp.cumsum(sigma, axis=1) - sigma
    trans = jnp.exp(-before)
    fade = jnp.exp(-sigma)
    weight = trans * -jnp.expm1(-sigma)
    weighted = weight[None] * colour
    seg_colour = jnp.sum(weighted, axis=2)
    seg_trans = jnp.exp(-jnp.sum(sigma, axis=1))
    blank = (jnp.zeros_like(seg_colour), jnp.ones_like(seg_trans))
    front_colour, front_trans = carried_in_2(
        (seg_colour, seg_trans), "depth", front_combine, blank, False
    )
    back_colour, back_trans = carried_in_2(
        (seg_colour, seg_trans), "depth", back_combine, blank, True
    )
    behind = back_colour + back_trans[None]
    pixel = front_colour + front_trans[None] * (seg_colour + seg_trans[None] * behind)
    pixel_grad = 0.5 * total_depth * (pixel - target)
    upto = jnp.cumsum(weighted, axis=2)
    remain = seg_colour[:, :, None, :] - upto + (seg_trans[None] * behind)[:, :, None, :]
    next_trans = trans * fade
    front_wide = front_trans[:, None, :]
    sigma_grad = front_wide * jnp.sum(
        pixel_grad[:, :, None, :] * (next_trans[None] * colour - remain), axis=0
    )
    colour_grad = front_wide[None] * weight[None] * pixel_grad[:, :, None, :]
    density_grad = sigma_grad * occ * scale * jax.nn.sigmoid(features[0])
    return jnp.concatenate([density_grad[None], colour_grad * colour * (1.0 - colour)], axis=0)


def expand_blocks(blocks):
    return jnp.repeat(jnp.repeat(jnp.repeat(blocks, 4, axis=0), 8, axis=1), 8, axis=2)


def body(grid, first_moment, second_moment, ray_offset, occupancy, target):
    depth_count = lax.axis_size("depth")
    planes = grid.shape[2]
    total_depth = planes * depth_count
    padded = with_halo(grid, (("tile", 1), ("depth", 2)), 1)
    shares = (ray_offset.astype(jnp.float32) * 0.5)[None, :, None, :]
    occ = expand_blocks(occupancy.astype(jnp.float32))
    feature_grad = render(grid, padded[:, 2:, 1:-1, :], shares, occ, target, total_depth)
    carried = shares * feature_grad
    incoming = passed_along(carried[:, -1:], "tile", 1)
    carried_in = jnp.concatenate([incoming, carried[:, :-1]], axis=1)
    data_grad = (1.0 - shares) * feature_grad + carried_in
    across_rows = padded[:, 2:, 1:-1, :] + padded[:, :-2, 1:-1, :]
    across_planes = padded[:, 1:-1, 2:, :] + padded[:, 1:-1, :-2, :]
    side_pad = jnp.pad(grid, ((0, 0), (0, 0), (0, 0), (1, 1)))
    across_cols = side_pad[:, :, :, 2:] + side_pad[:, :, :, :-2]
    smooth_grad = 2.0 * tv_weight * (6.0 * grid - across_rows - across_planes - across_cols)
    grad = data_grad + smooth_grad
    new_first = beta_one * first_moment + (1.0 - beta_one) * grad
    new_second = beta_two * second_moment + (1.0 - beta_two) * grad * grad
    corr_one = 1.0 - beta_one**adam_step
    corr_two = 1.0 - beta_two**adam_step
    new_grid = grid - learn_rate * (new_first / corr_one) / (
        jnp.sqrt(new_second / corr_two) + epsilon
    )
    return (new_grid, new_first, new_second)


def solution(mesh):
    in_specs = (
        P(None, "tile", "depth", None),
        P(None, "tile", "depth", None),
        P(None, "tile", "depth", None),
        P("tile", None),
        P("tile", "depth", None),
        P(None, "tile", None),
    )
    out_specs = (
        P(None, "tile", "depth", None),
        P(None, "tile", "depth", None),
        P(None, "tile", "depth", None),
    )
    return jax.shard_map(body, mesh=mesh, in_specs=in_specs, out_specs=out_specs, check_vma=False)
```

profile of v0, /device:TPU:4, one launch (start us, length us, event | category | flops | bytes accessed | tf_op | source)
XLA Modules:
  0.0 59.3 jit_solution(14934395197131300803)
XLA Ops:
  0.6 1.0 %fusion.28 = (f32[4,1,8,1024]{3,2,1,0:T(8,128)S(1)}, f32[4,1,8,1024]{3,2,1,0:T(8,128)S(1)}) fusion(f32[4,4,8,1024]{3,2,1,0:T(8,128)} %param.10), kind=kLoop, calls=%fused_computation.63 | loop fusion | bytes 524288 | tf_op jit(solution)/shard_map/slice | solution.py:35
  1.7 2.8 %collective-permute-start = (f32[4,1,8,1024]{3,2,1,0:T(8,128)S(1)}, f32[4,1,8,1024]{3,2,1,0:T(8,128)S(1)}, u32[]{:S(2)}, u32[]{:S(2)}) collective-permute-start(f32[4,1,8,1024]{3,2,1,0:T(8,128)S(1)} %get-tuple-element.315), channel_id=1, source_target_pairs={{4,0},{8,4},{12,8},{16,12},{20,16},{24,20},{28,24},{5,1},{9,5},{13... | collective-permute-start | bytes 393224 | tf_op jit(solution)/shard_map/ppermute | solution.py:41
  4.5 1.9 %collective-permute-start.2 = (f32[4,1,8,1024]{3,2,1,0:T(8,128)S(1)}, f32[4,1,8,1024]{3,2,1,0:T(8,128)S(1)}, u32[]{:S(2)}, u32[]{:S(2)}) collective-permute-start(f32[4,1,8,1024]{3,2,1,0:T(8,128)S(1)} %get-tuple-element.316), channel_id=1, source_target_pairs={{0,4},{4,8},{8,12},{12,16},{16,20},{20,24},{24,28},{1,5},{5,9},{9,... | collective-permute-start | bytes 393224 | tf_op jit(solution)/shard_map/ppermute | solution.py:39
  6.4 0.7 %broadcast_subtract_fusion = (f32[4,1024]{1,0:T(4,128)S(1)}, f32[4,1024]{1,0:T(4,128)S(1)}) fusion(s32[4,1024]{1,0:T(4,128)} %param.13), kind=kLoop, calls=%fused_computation.57 | loop fusion | flops 12288 | bytes 49152 | tf_op jit(solution)/shard_map/sub | solution.py:111
  7.4 4.3 %collective-permute-done.2 = f32[4,1,8,1024]{3,2,1,0:T(8,128)S(1)} collective-permute-done((f32[4,1,8,1024]{3,2,1,0:T(8,128)S(1)}, f32[4,1,8,1024]{3,2,1,0:T(8,128)S(1)}, u32[]{:S(2)}, u32[]{:S(2)}) %collective-permute-start.2) | collective-permute-done | bytes 131104 | tf_op jit(solution)/shard_map/ppermute | solution.py:39
  11.7 0.6 %copy-done.2 = f32[4,1,8,1024]{3,2,1,0:T(8,128)} copy-done((f32[4,1,8,1024]{3,2,1,0:T(8,128)}, f32[4,1,8,1024]{3,2,1,0:T(8,128)S(1)}, u32[]{:S(2)}) %copy-start.2) | copy-done | bytes 131096
  12.6 0.6 %negate_exponential_fusion.1 = (f32[4,1024]{1,0:T(4,128)}, f32[1,4,1024]{2,1,0:T(4,128)S(1)}) fusion(f32[4,1024]{1,0:T(4,128)S(1)} %get-tuple-element.305), kind=kLoop, calls=%fused_computation.51 | loop fusion | flops 4096 | bytes 49152 | tf_op jit(solution)/shard_map/exp | solution.py:73
  13.2 13.4 %all-gather.2 = f32[4,4,1024]{2,1,0:T(4,128)S(1)} all-gather(f32[1,4,1024]{2,1,0:T(4,128)S(1)} %get-tuple-element.320), channel_id=3, replica_groups=mesh['tile'=8,'depth'=4] {'depth'}, dimensions={0}, use_global_device_ids=true | all-gather | bytes 81920 | tf_op jit(solution)/shard_map/all_gather | solution.py:16
  26.8 0.2 fusion.26
  27.0 0.3 reduce_window_sum.23
  27.3 13.7 %all-gather = f32[12,4,1024]{2,1,0:T(4,128)S(1)} all-gather(f32[3,4,1024]{2,1,0:T(4,128)S(1)} %get-tuple-element.307), channel_id=2, replica_groups=mesh['tile'=8,'depth'=4] {'depth'}, dimensions={0}, use_global_device_ids=true | all-gather | bytes 245760 | tf_op jit(solution)/shard_map/all_gather | solution.py:16
  41.0 0.3 while.32
  41.3 0.7 %multiply_bitcast_fusion.1 = (f32[4,8,1024]{2,1,0:T(8,128)S(1)}, f32[4,8,1024]{2,1,0:T(8,128)}) fusion(f32[1,4,8,1024]{3,2,1,0:T(8,128)S(1)} %get-tuple-element.306, f32[1,4,8,1024]{3,2,1,0:T(8,128)S(1)} %reduce_window_sum.22, f32[4,1024]{1,0:T(4,128)S(1)} %get-tuple-element.223), kind=kLoop, calls=%fused_computation.46 | loop fusion | flops 229376 | bytes 540672 | tf_op jit(solution)/shard_map/mul | solution.py:89
  42.0 0.2 while.33
  42.3 0.5 copy-done.7
  42.9 0.9 %copy-done.4 = f32[4,8,1024]{2,1,0:T(8,128)S(1)} copy-done((f32[4,8,1024]{2,1,0:T(8,128)S(1)}, f32[4,8,1024]{2,1,0:T(8,128)}, u32[]{:S(2)}) %copy-start.4) | copy-done | bytes 131096
  43.8 0.2 multiply_reduce_fusion
  44.0 0.5 copy-done.10
  44.6 1.9 %collective-permute-start.1 = (f32[4,1,8,1024]{3,2,1,0:T(8,128)S(1)}, f32[4,1,8,1024]{3,2,1,0:T(8,128)S(1)}, u32[]{:S(2)}, u32[]{:S(2)}) collective-permute-start(f32[4,1,8,1024]{3,2,1,0:T(8,128)S(1)} %slice.64), channel_id=1, source_target_pairs={{0,4},{4,8},{8,12},{12,16},{16,20},{20,24},{24,28},{1,5},{5,9},{9,... | collective-permute-start | bytes 393224 | tf_op jit(solution)/shard_map/ppermute | solution.py:51
  46.7 3.5 %collective-permute-start.4 = (f32[4,6,1,1024]{3,1,2,0:T(8,128)S(1)}, f32[4,6,1,1024]{3,1,2,0:T(8,128)S(1)}, u32[]{:S(2)}, u32[]{:S(2)}) collective-permute-start(f32[4,6,1,1024]{3,1,2,0:T(8,128)S(1)} %copy.25), channel_id=1, source_target_pairs={{0,1},{1,2},{2,3},{4,5},{5,6},{6,7},{8,9},{9,10},{10,11},{12,13},{... | collective-permute-start | bytes 294920 | tf_op jit(solution)/shard_map/ppermute | solution.py:39
  50.3 1.4 %collective-permute-start.3 = (f32[4,6,1,1024]{3,1,2,0:T(8,128)S(1)}, f32[4,6,1,1024]{3,1,2,0:T(8,128)S(1)}, u32[]{:S(2)}, u32[]{:S(2)}) collective-permute-start(f32[4,6,1,1024]{3,1,2,0:T(8,128)S(1)} %copy.23), channel_id=1, source_target_pairs={{1,0},{2,1},{3,2},{5,4},{6,5},{7,6},{9,8},{10,9},{11,10},{13,12},{... | collective-permute-start | bytes 294920 | tf_op jit(solution)/shard_map/ppermute | solution.py:41
  51.7 1.2 %collective-permute-done.4 = f32[4,6,1,1024]{3,1,2,0:T(8,128)S(1)} collective-permute-done((f32[4,6,1,1024]{3,1,2,0:T(8,128)S(1)}, f32[4,6,1,1024]{3,1,2,0:T(8,128)S(1)}, u32[]{:S(2)}, u32[]{:S(2)}) %collective-permute-start.4) | collective-permute-done | bytes 98336 | tf_op jit(solution)/shard_map/ppermute | solution.py:39
  53.1 4.2 %collective-permute-done.3 = f32[4,6,1,1024]{3,1,2,0:T(8,128)S(1)} collective-permute-done((f32[4,6,1,1024]{3,1,2,0:T(8,128)S(1)}, f32[4,6,1,1024]{3,1,2,0:T(8,128)S(1)}, u32[]{:S(2)}, u32[]{:S(2)}) %collective-permute-start.3) | collective-permute-done | bytes 98336 | tf_op jit(solution)/shard_map/ppermute | solution.py:41
  57.4 1.9 %divide_subtract_fusion = (f32[4,4,8,1024]{3,2,1,0:T(8,128)}, f32[4,4,8,1024]{3,2,1,0:T(8,128)}, f32[4,4,8,1024]{3,2,1,0:T(8,128)}) fusion(f32[4,4,8,1024]{3,2,1,0:T(8,128)S(1)} %copy-done, f32[4,4,8,1024]{3,2,1,0:T(8,128)S(1)} %copy-done.5, f32[4,4,8,1024]{3,2,1,0:T(8,128)S(1)} %copy-done.6, f32[4,6,8,1024]{3,2,1,0:T(8,128)S(1)} %constant_dynamic-update-slice_fusion, ...), kind=kLoop, calls=%fused_computation.28 | loop fusion | flops 3801088 | bytes 5455872 | tf_op jit(solution)/shard_map/sub | solution.py:122
  (60 shorter events, 1.7 us)
Async XLA Ops:
  0.6 11.7 %copy-start = (f32[4,4,8,1024]{3,2,1,0:T(8,128)S(1)}, f32[4,4,8,1024]{3,2,1,0:T(8,128)}, u32[]{:S(2)}) copy-start(f32[4,4,8,1024]{3,2,1,0:T(8,128)} %param.10) | copy-start | bytes 1572868
  1.7 10.0 %collective-permute-start = (f32[4,1,8,1024]{3,2,1,0:T(8,128)S(1)}, f32[4,1,8,1024]{3,2,1,0:T(8,128)S(1)}, u32[]{:S(2)}, u32[]{:S(2)}) collective-permute-start(f32[4,1,8,1024]{3,2,1,0:T(8,128)S(1)} %get-tuple-element.315), channel_id=1, source_target_pairs={{4,0},{8,4},{12,8},{16,12},{20,16},{24,20},{28,24},{5,1},{9,5},{13... | collective-permute-start | bytes 393224 | tf_op jit(solution)/shard_map/ppermute | solution.py:41
  4.5 2.7 %copy-start.11 = (s32[1,1,128]{2,1,0:T(1,128)S(1)}, s32[1,1,128]{2,1,0:T(1,128)}, u32[]{:S(2)}) copy-start(s32[1,1,128]{2,1,0:T(1,128)} %param.14) | copy-start | bytes 1540
  4.5 7.2 %collective-permute-start.2 = (f32[4,1,8,1024]{3,2,1,0:T(8,128)S(1)}, f32[4,1,8,1024]{3,2,1,0:T(8,128)S(1)}, u32[]{:S(2)}, u32[]{:S(2)}) collective-permute-start(f32[4,1,8,1024]{3,2,1,0:T(8,128)S(1)} %get-tuple-element.316), channel_id=1, source_target_pairs={{0,4},{4,8},{8,12},{12,16},{16,20},{20,24},{24,28},{1,5},{5,9},{9,... | collective-permute-start | bytes 393224 | tf_op jit(solution)/shard_map/ppermute | solution.py:39
  7.4 5.0 %copy-start.9 = (f32[1024]{0:T(1024)}, f32[1024]{0:T(1024)S(1)}, u32[]{:S(2)}) copy-start(f32[1024]{0:T(1024)S(1)} %broadcast_in_dim.13) | copy-start | bytes 12292
  11.7 0.7 %copy-start.2 = (f32[4,1,8,1024]{3,2,1,0:T(8,128)}, f32[4,1,8,1024]{3,2,1,0:T(8,128)S(1)}, u32[]{:S(2)}) copy-start(f32[4,1,8,1024]{3,2,1,0:T(8,128)S(1)} %collective-permute-done.2) | copy-start | bytes 393220
  42.0 0.7 %copy-start.7 = (f32[4,1024]{1,0:T(4,128)S(1)}, f32[4,1024]{1,0:T(4,128)}, u32[]{:S(2)}) copy-start(f32[4,1024]{1,0:T(4,128)} %get-tuple-element.319) | copy-start | bytes 49156
  42.0 0.8 %copy-start.8 = (f32[3,4,1024]{2,1,0:T(4,128)S(1)}, f32[3,4,1024]{2,1,0:T(4,128)}, u32[]{:S(2)}) copy-start(f32[3,4,1024]{2,1,0:T(4,128)} %param.15) | copy-start | bytes 147460
  42.9 0.9 %copy-start.4 = (f32[4,8,1024]{2,1,0:T(8,128)S(1)}, f32[4,8,1024]{2,1,0:T(8,128)}, u32[]{:S(2)}) copy-start(f32[4,8,1024]{2,1,0:T(8,128)} %get-tuple-element.318) | copy-start | bytes 393220
  43.8 0.7 %copy-start.10 = (f32[1024]{0:T(1024)S(1)}, f32[1024]{0:T(1024)}, u32[]{:S(2)}) copy-start(f32[1024]{0:T(1024)} %copy-done.9) | copy-start | bytes 12292
  44.6 7.2 %copy-start.1 = (f32[4,4,8,1024]{3,2,1,0:T(8,128)}, f32[4,4,8,1024]{3,2,1,0:T(8,128)S(1)}, u32[]{:S(2)}) copy-start(f32[4,4,8,1024]{3,2,1,0:T(8,128)S(1)} %fusion.12) | copy-start | bytes 1572868
  44.6 12.8 %collective-permute-start.1 = (f32[4,1,8,1024]{3,2,1,0:T(8,128)S(1)}, f32[4,1,8,1024]{3,2,1,0:T(8,128)S(1)}, u32[]{:S(2)}, u32[]{:S(2)}) collective-permute-start(f32[4,1,8,1024]{3,2,1,0:T(8,128)S(1)} %slice.64), channel_id=1, source_target_pairs={{0,4},{4,8},{8,12},{12,16},{16,20},{20,24},{24,28},{1,5},{5,9},{9,... | collective-permute-start | bytes 393224 | tf_op jit(solution)/shard_map/ppermute | solution.py:51
  46.7 10.7 %copy-start.6 = (f32[4,4,8,1024]{3,2,1,0:T(8,128)S(1)}, f32[4,4,8,1024]{3,2,1,0:T(8,128)}, u32[]{:S(2)}) copy-start(f32[4,4,8,1024]{3,2,1,0:T(8,128)} %param.12) | copy-start | bytes 1572868
  46.7 6.2 %collective-permute-start.4 = (f32[4,6,1,1024]{3,1,2,0:T(8,128)S(1)}, f32[4,6,1,1024]{3,1,2,0:T(8,128)S(1)}, u32[]{:S(2)}, u32[]{:S(2)}) collective-permute-start(f32[4,6,1,1024]{3,1,2,0:T(8,128)S(1)} %copy.25), channel_id=1, source_target_pairs={{0,1},{1,2},{2,3},{4,5},{5,6},{6,7},{8,9},{9,10},{10,11},{12,13},{... | collective-permute-start | bytes 294920 | tf_op jit(solution)/shard_map/ppermute | solution.py:39
  50.3 7.1 %copy-start.5 = (f32[4,4,8,1024]{3,2,1,0:T(8,128)S(1)}, f32[4,4,8,1024]{3,2,1,0:T(8,128)}, u32[]{:S(2)}) copy-start(f32[4,4,8,1024]{3,2,1,0:T(8,128)} %param.11) | copy-start | bytes 1572868
  50.3 7.0 %collective-permute-start.3 = (f32[4,6,1,1024]{3,1,2,0:T(8,128)S(1)}, f32[4,6,1,1024]{3,1,2,0:T(8,128)S(1)}, u32[]{:S(2)}, u32[]{:S(2)}) collective-permute-start(f32[4,6,1,1024]{3,1,2,0:T(8,128)S(1)} %copy.23), channel_id=1, source_target_pairs={{1,0},{2,1},{3,2},{5,4},{6,5},{7,6},{9,8},{10,9},{11,10},{13,12},{... | collective-permute-start | bytes 294920 | tf_op jit(solution)/shard_map/ppermute | solution.py:41
  51.7 5.7 %copy-start.3 = (f32[4,1,8,1024]{3,2,1,0:T(8,128)S(1)}, f32[4,1,8,1024]{3,2,1,0:T(8,128)}, u32[]{:S(2)}) copy-start(f32[4,1,8,1024]{3,2,1,0:T(8,128)} %copy-done.2) | copy-start | bytes 393220
  51.7 5.7 %slice-start = ((f32[4,4,8,1024]{3,2,1,0:T(8,128)}), f32[4,3,8,1024]{3,2,1,0:T(8,128)S(1)}, s32[]{:S(2)}) async-start(f32[4,4,8,1024]{3,2,1,0:T(8,128)} %copy-done.1), calls=%async_computation | async-start | bytes 786432 | tf_op jit(solution)/shard_map/slice | solution.py:110
where the time goes:
time: 60.1 us; the launch traced here: 59.3 us
  blocking collectives  27.1 us (45%)
  starting transfers between devices  11.6 us (19%)
  waiting for transfers between devices  9.71 us (16%)
  other arithmetic  5.62 us (9%)
  local copies, waits for them, and re-layouts  4.24 us (7%)
  between operations  0.98 us (2%)
    all_gather x2, blocking collectives, carried_in_2(): pieces = jax.tree.map(lambda part: lax.all_gather(part, axis), value)  27.1 us
    ppermute x2, waiting for transfers between devices, with_halo(): lax.ppermute(tail, axis, [(i, (i + 1) % count) for i in range(ends)])  5.49 us
    ppermute x2, starting transfers between devices, with_halo(): lax.ppermute(tail, axis, [(i, (i + 1) % count) for i in range(ends)])  5.43 us
    ppermute x2, waiting for transfers between devices, with_halo(): lax.ppermute(head, axis, [((i + 1) % count, i) for i in range(ends)])  4.22 us
    ppermute x2, starting transfers between devices, with_halo(): lax.ppermute(head, axis, [((i + 1) % count, i) for i in range(ends)])  4.21 us
    unnamed x25, local copies, waits for them, and re-layouts  2.6 us
    ppermute x1, starting transfers between devices, passed_along(): return lax.ppermute(block, axis, route)  1.92 us
    sub x1, other arithmetic, body(): grid - learn_rate * (new_first / corr_one) / (jnp.sqrt(new_second / corr_...  1.91 us
  transfers between devices with their start and end apart: 5, of which 3 were waited for; matrix products, arithmetic and copies ran while one was open for 2% of the time, Pallas kernels for 0%

commit v1 on v0

v1 whole, which is shorter than its diff:
```python
import functools

import jax
import jax.numpy as jnp
from jax import lax
from jax.experimental import pallas as pl
from jax.experimental.pallas import tpu as pltpu
from jax.sharding import PartitionSpec as P

MESH = pl.DeviceIdType.MESH
tv_weight = 0.01
beta_one = 0.9
beta_two = 0.95
learn_rate = 0.1
adam_step = 10
epsilon = 1e-08


def running_sum(x, iota, backward):
    count = x.shape[0]
    step = 1
    while step < count:
        if backward:
            x = x + jnp.where(iota < count - step, pltpu.roll(x, count - step, 0), 0.0)
        else:
            x = x + jnp.where(iota >= step, pltpu.roll(x, step, 0), 0.0)
        step *= 2
    return x


def one_minus_exp(s):
    series = 1.0 / 120 - s * (1.0 / 720)
    for term in (1.0 / 24, 1.0 / 6, 0.5, 1.0):
        series = term - s * series
    return jnp.where(s < 0.25, s * series, 1.0 - jnp.exp(-s))


def sigmoid(x):
    return 1.0 / (1.0 + jnp.exp(-x))


def kernel(
    tiles, depths, pieces,
    grid_h, ray_h, occ_h, tgt_h, grad_ref,
    g, ray, occ_i, tgt, nxt, prv, ext_out, ext_in, zout, zin,
    col, wgt, ntr, dfac,
    seg1_out, seg1_in, seg2_out, seg2_in,
    qd1_out, qd1_in, qd2_out, qd2_in, qdp_in,
    load_sem, halo_send, halo_recv,
    s1_send, s1_recv, s2_send, s2_recv,
    q1_send, q1_recv, q2_send, q2_recv, qp_send, qp_recv,
):
    t, k = lax.axis_index("tile"), lax.axis_index("depth")
    channels, rows, planes, width = g.shape
    last = rows - 1
    piece = width // pieces
    scale = 4.0 / (planes * depths)
    has_prev, has_next = t > 0, t < tiles - 1
    reduces = k < pieces

    loads = [
        pltpu.make_async_copy(src, dst, load_sem.at[i])
        for i, (src, dst) in enumerate(((grid_h, g), (ray_h, ray), (occ_h, occ_i), (tgt_h, tgt)))
    ]
    for load in loads:
        load.start()

    barrier = pltpu.get_barrier_semaphore()
    for d in range(1, depths):
        pl.semaphore_signal(barrier, inc=1, device_id={"depth": lax.rem(k + d, depths)}, device_id_type=MESH)

    @pl.when(has_prev)
    def _():
        for j in range(depths):
            pl.semaphore_signal(barrier, inc=1, device_id={"tile": t - 1, "depth": j}, device_id_type=MESH)

    @pl.when(has_next)
    def _():
        for j in range(depths):
            pl.semaphore_signal(barrier, inc=1, device_id={"tile": t + 1, "depth": j}, device_id_type=MESH)

    @pl.when(jnp.logical_not(has_prev))
    def _():
        prv[...] = jnp.zeros_like(prv)
        ext_in[...] = jnp.zeros_like(ext_in)
        qdp_in[...] = jnp.zeros_like(qdp_in)

    @pl.when(jnp.logical_not(has_next))
    def _():
        nxt[...] = jnp.zeros_like(nxt)

    @pl.when(k == 0)
    def _():
        zin[0] = jnp.zeros(zin.shape[1:], jnp.float32)

    @pl.when(k == depths - 1)
    def _():
        zin[1] = jnp.zeros(zin.shape[1:], jnp.float32)

    for load in loads:
        load.wait()

    blocks = occ_i.shape[2]
    spread = lax.broadcasted_iota(jnp.int32, (blocks, width), 1) // (width // blocks)
    spread = (spread == lax.broadcasted_iota(jnp.int32, (blocks, width), 0)).astype(jnp.float32)
    occ_rows = jnp.broadcast_to(occ_i[0].astype(jnp.float32), (8, blocks))
    occ = jnp.dot(occ_rows, spread, preferred_element_type=jnp.float32)[0:1]
    ext_out[0:1, :] = ray[last : last + 1, :].astype(jnp.float32) * 0.5
    ext_out[1:2, :] = occ
    for c in range(channels):
        for r in range(rows):
            zout[0, c * rows + r : c * rows + r + 1, :] = g[c, r, planes - 1 : planes, :]
            zout[1, c * rows + r : c * rows + r + 1, :] = g[c, r, 0:1, :]

    to_prev = pltpu.make_async_remote_copy(
        g.at[:, 0:1], nxt, halo_send.at[0], halo_recv.at[0], device_id={"tile": t - 1}, device_id_type=MESH
    )
    to_next = pltpu.make_async_remote_copy(
        g.at[:, last:rows], prv, halo_send.at[1], halo_recv.at[1], device_id={"tile": t + 1}, device_id_type=MESH
    )
    ext_next = pltpu.make_async_remote_copy(
        ext_out, ext_in, halo_send.at[2], halo_recv.at[2], device_id={"tile": t + 1}, device_id_type=MESH
    )
    z_back = pltpu.make_async_remote_copy(
        zout.at[0], zin.at[0], halo_send.at[3], halo_recv.at[3], device_id={"depth": k + 1}, device_id_type=MESH
    )
    z_front = pltpu.make_async_remote_copy(
        zout.at[1], zin.at[1], halo_send.at[4], halo_recv.at[4], device_id={"depth": k - 1}, device_id_type=MESH
    )

    partners = depths - 1 + depths * (has_prev.astype(jnp.int32) + has_next.astype(jnp.int32))
    pl.semaphore_wait(barrier, partners)

    @pl.when(has_prev)
    def _():
        to_prev.start()

    @pl.when(has_next)
    def _():
        to_next.start()
        ext_next.start()

    @pl.when(k < depths - 1)
    def _():
        z_back.start()

    @pl.when(k > 0)
    def _():
        z_front.start()

    planes_at = lax.broadcasted_iota(jnp.int32, (planes, width), 0)

    def samples(slot, here, after, share, occ):
        density = here(0) + share * (after(0) - here(0))
        tail = jnp.exp(-jnp.abs(density))
        sigma = occ * (jnp.maximum(density, 0.0) + jnp.log1p(tail)) * scale
        dfac[slot] = occ * scale * jnp.where(density >= 0.0, 1.0, tail) / (1.0 + tail)
        upto = running_sum(sigma, planes_at, False)
        weight = jnp.exp(sigma - upto) * one_minus_exp(sigma)
        after_all = jnp.exp(-upto)
        wgt[slot] = weight
        ntr[slot] = after_all
        out = []
        for c in range(1, channels):
            colour = sigmoid(here(c) + share * (after(c) - here(c)))
            col[slot, c - 1] = colour
            out.append(jnp.sum(weight * colour, axis=0, keepdims=True))
        out.append(after_all[planes - 1 : planes])
        return out

    def share_of(r):
        return ray[r : r + 1, :].astype(jnp.float32) * 0.5

    def put(seg_out, r, values):
        for v in range(channels):
            for p in range(pieces):
                seg_out[p, v, r : r + 1, :] = values[v][:, p * piece : (p + 1) * piece]

    def when_reduces(who, work):
        if pieces < depths:
            pl.when(who < pieces)(work)
        else:
            work()

    def seg_copy(seg_out, seg_in, send, recv, d, source=None):
        to = lax.rem(k + d, depths)
        slot = k if source is None else source
        return pltpu.make_async_remote_copy(
            seg_out.at[to % pieces], seg_in.at[slot], send.at[d], recv.at[slot],
            device_id={"depth": to}, device_id_type=MESH,
        )

    def send_segments(seg_out, seg_in, send, recv):
        for d in range(1, depths):
            when_reduces(lax.rem(k + d, depths), seg_copy(seg_out, seg_in, send, recv, d).start)

        def own():
            seg_in[k] = seg_out[k % pieces]

        when_reduces(k, own)

    def reduce(seg_in, qd_out, send, recv, first, count):
        for d in range(1, depths):
            source = lax.rem(k + d, depths)
            seg_copy(seg_in, seg_in, send, recv, d, source).wait_recv()
        at = pl.ds(pl.multiple_of((k % pieces) * piece, piece), piece)
        fronts = [None]
        front = seg_in[0, 3]
        pixel = [seg_in[0, c] for c in range(3)]
        fronts.append(front)
        for j in range(1, depths):
            for c in range(3):
                pixel[c] = pixel[c] + front * seg_in[j, c]
            front = front * seg_in[j, 3]
            fronts.append(front)
        half = 0.5 * planes * depths
        pg = [half * (pixel[c] + front - tgt[c, first : first + count, at]) for c in range(3)]
        behind = pg[0] + pg[1] + pg[2]
        for j in range(depths - 1, -1, -1):
            for c in range(3):
                qd_out[j, c] = pg[c] if j == 0 else fronts[j] * pg[c]
            qd_out[j, 3] = fronts[j + 1] * behind
            if j:
                behind = pg[0] * seg_in[j, 0] + pg[1] * seg_in[j, 1] + pg[2] * seg_in[j, 2] + seg_in[j, 3] * behind

    def qd_copy(qd_out, qd_in, send, recv, d, source=None):
        to = lax.rem(k + d, depths)
        slot = k % pieces if source is None else source % pieces
        return pltpu.make_async_remote_copy(
            qd_out.at[to], qd_in.at[slot], send.at[d], recv.at[slot],
            device_id={"depth": to}, device_id_type=MESH,
        )

    def qd_copy_next(d, source=None):
        to = lax.rem(k + d, depths)
        slot = k % pieces if source is None else source % pieces
        return pltpu.make_async_remote_copy(
            qd2_out.at[to], qdp_in.at[slot], qp_send.at[d], qp_recv.at[slot],
            device_id={"tile": t + 1, "depth": to}, device_id_type=MESH,
        )

    def send_back(qd_out, qd_in, send, recv):
        for d in range(1, depths):
            qd_copy(qd_out, qd_in, send, recv, d).start()
        qd_in[k % pieces] = qd_out[k]

    def wait_back(qd_in, send, recv):
        for d in range(1, depths):
            source = lax.rem(k + d, depths)
            when_reduces(source, qd_copy(qd_in, qd_in, send, recv, d, source).wait_recv)

    for r in range(last):
        values = samples(r, lambda c: g[c, r], lambda c: g[c, r + 1], share_of(r), occ)
        put(seg1_out, r, values)
    send_segments(seg1_out, seg1_in, s1_send, s1_recv)

    pl.when(has_next)(to_prev.wait_recv)
    values = samples(last, lambda c: g[c, last], lambda c: nxt[c, 0], share_of(last), occ)
    put(seg2_out, 0, values)
    send_segments(seg2_out, seg2_in, s2_send, s2_recv)

    def first_rows():
        reduce(seg1_in, qd1_out, s1_send, s1_recv, 0, last)
        send_back(qd1_out, qd1_in, q1_send, q1_recv)

    when_reduces(k, first_rows)

    def last_row():
        reduce(seg2_in, qd2_out, s2_send, s2_recv, last, 1)
        send_back(qd2_out, qd2_in, q2_send, q2_recv)

        @pl.when(has_next)
        def _():
            for d in range(depths):
                qd_copy_next(d).start()

    when_reduces(k, last_row)

    @pl.when(has_prev)
    def _():
        to_next.wait_recv()
        ext_next.wait_recv()

    samples(rows, lambda c: prv[c, 0], lambda c: g[c, 0], ext_in[0:1, :], ext_in[1:2, :])

    pl.when(k > 0)(z_back.wait_recv)
    pl.when(k < depths - 1)(z_front.wait_recv)
    lanes = lax.broadcasted_iota(jnp.int32, (planes, width), 1)
    for c in range(channels):
        for r in range(rows):
            here = g[c, r]
            i = c * rows + r
            around = (prv[c, 0] if r == 0 else g[c, r - 1]) + (nxt[c, 0] if r == last else g[c, r + 1])
            around += jnp.where(planes_at == 0, zin[0, i : i + 1, :], pltpu.roll(here, 1, 0))
            around += jnp.where(planes_at == planes - 1, zin[1, i : i + 1, :], pltpu.roll(here, planes - 1, 0))
            around += jnp.where(lanes == 0, 0.0, pltpu.roll(here, 1, 1))
            around += jnp.where(lanes == width - 1, 0.0, pltpu.roll(here, width - 1, 1))
            grad_ref[c, r] = 2.0 * tv_weight * (6.0 * here - around)

    def gradient(slot, qd_in, r):
        q = [jnp.concatenate([qd_in[p, v, r : r + 1, :] for p in range(pieces)], axis=1) for v in range(4)]
        u = q[0] * col[slot, 0] + q[1] * col[slot, 1] + q[2] * col[slot, 2]
        weight = wgt[slot]
        part = weight * u
        rest = running_sum(part, planes_at, True) - part
        out = [(ntr[slot] * u - rest - q[3]) * dfac[slot]]
        for c in range(3):
            colour = col[slot, c]
            out.append(q[c] * weight * (colour * (1.0 - colour)))
        return out

    def add(r, factor, values):
        for c in range(channels):
            grad_ref[c, r] += factor * values[c]

    wait_back(qd1_in, q1_send, q1_recv)
    for r in range(last):
        values = gradient(r, qd1_in, r)
        add(r, 1.0 - share_of(r), values)
        add(r + 1, share_of(r), values)
    wait_back(qd2_in, q2_send, q2_recv)
    add(last, 1.0 - share_of(last), gradient(last, qd2_in, 0))

    @pl.when(has_prev)
    def _():
        for d in range(depths):
            source = lax.rem(k + d, depths)
            when_reduces(source, qd_copy_next(d, source).wait_recv)

    add(0, ext_in[0:1, :], gradient(rows, qdp_in, 0))

    pl.when(has_prev)(to_prev.wait_send)

    @pl.when(has_next)
    def _():
        to_next.wait_send()
        ext_next.wait_send()

    pl.when(k < depths - 1)(z_back.wait_send)
    pl.when(k > 0)(z_front.wait_send)
    for d in range(1, depths):
        to = lax.rem(k + d, depths)
        when_reduces(to, seg_copy(seg1_out, seg1_in, s1_send, s1_recv, d).wait_send)
        when_reduces(to, seg_copy(seg2_out, seg2_in, s2_send, s2_recv, d).wait_send)

    def sent_back():
        for d in range(1, depths):
            qd_copy(qd1_out, qd1_in, q1_send, q1_recv, d).wait_send()
            qd_copy(qd2_out, qd2_in, q2_send, q2_recv, d).wait_send()

        @pl.when(has_next)
        def _():
            for d in range(depths):
                qd_copy_next(d).wait_send()

    when_reduces(k, sent_back)


def gradient_of_loss(grid, ray_offset, occupancy, target, tiles, depths):
    channels, rows, planes, width = grid.shape
    pieces = max(1, min(depths, width // 128))
    piece = width // pieces
    f32 = jnp.float32
    vmem, dma = pltpu.VMEM, pltpu.SemaphoreType.DMA
    scratch = [
        vmem(grid.shape, f32), vmem(ray_offset.shape, jnp.int32), vmem(occupancy.shape, jnp.int32),
        vmem(target.shape, f32),
        vmem((channels, 1, planes, width), f32), vmem((channels, 1, planes, width), f32),
        vmem((8, width), f32), vmem((8, width), f32),
        vmem((2, channels * rows, width), f32), vmem((2, channels * rows, width), f32),
        vmem((rows + 1, 3, planes, width), f32), vmem((rows + 1, planes, width), f32),
        vmem((rows + 1, planes, width), f32), vmem((rows + 1, planes, width), f32),
    ]
    for count in (rows - 1, 1):
        scratch += [vmem((pieces, 4, count, piece), f32), vmem((depths, 4, count, piece), f32)]
    for count in (rows - 1, 1):
        scratch += [vmem((depths, 4, count, piece), f32), vmem((pieces, 4, count, piece), f32)]
    scratch += [vmem((pieces, 4, 1, piece), f32)]
    scratch += [dma((4,)), dma((5,)), dma((5,))] + [dma((depths,))] * 10
    hbm = pl.BlockSpec(memory_space=pl.ANY)
    return pl.pallas_call(
        functools.partial(kernel, tiles, depths, pieces),
        out_shape=jax.ShapeDtypeStruct(grid.shape, f32),
        in_specs=[hbm] * 4,
        out_specs=pl.BlockSpec(memory_space=pltpu.VMEM),
        scratch_shapes=scratch,
        compiler_params=pltpu.CompilerParams(
            collective_id=0, has_side_effects=True, vmem_limit_bytes=24 * 2**20
        ),
        cost_estimate=pl.CostEstimate(flops=10**7, bytes_accessed=2**20, transcendentals=10**6),
    )(grid, ray_offset, occupancy, target)


def solution(mesh):
    tiles, depths = mesh.shape["tile"], mesh.shape["depth"]
    voxels = P(None, "tile", "depth", None)
    in_specs = (voxels, voxels, voxels, P("tile", None), P("tile", "depth", None), P(None, "tile", None))

    def body(grid, first_moment, second_moment, ray_offset, occupancy, target):
        grad = gradient_of_loss(grid, ray_offset, occupancy, target, tiles, depths)
        new_first = beta_one * first_moment + (1.0 - beta_one) * grad
        new_second = beta_two * second_moment + (1.0 - beta_two) * grad * grad
        corr_one = 1.0 - beta_one**adam_step
        corr_two = 1.0 - beta_two**adam_step
        new_grid = grid - learn_rate * (new_first / corr_one) / (jnp.sqrt(new_second / corr_two) + epsilon)
        return (new_grid, new_first, new_second)

    return jax.shard_map(body, mesh=mesh, in_specs=in_specs, out_specs=(voxels,) * 3, check_vma=False)
```

time: 60.1 us -> 22.5 us (0.37)
  blocking collectives: 27.1 us -> 0 us
  Pallas kernels: 0 us -> 17 us
  starting transfers between devices: 11.6 us -> 0 us
  waiting for transfers between devices: 9.71 us -> 0 us
  other arithmetic: 5.62 us -> 1.36 us
  local copies, waits for them, and re-layouts: 4.24 us -> 3.21 us
    all_gather x2 -> x0, blocking collectives: 27.1 us -> none  [carried_in_2(): pieces = jax.tree.map(lambda part: lax.all_gather(part, axis), value)]
    pallas_call x0 -> x1, Pallas kernels: none -> 17 us  [gradient_of_loss(): pl.pallas_call(functools.partial(kernel, tiles, depths, pieces), out_shap...]
    ppermute x5 -> x0, starting transfers between devices: 11.6 us -> none  [the longest x2 5.43 us: with_halo(): lax.ppermute(tail, axis, [(i, (i + 1) % count) for i in range(ends)])]
    ppermute x5 -> x0, waiting for transfers between devices: 9.71 us -> none  [the longest x2 5.49 us: with_halo(): lax.ppermute(tail, axis, [(i, (i + 1) % count) for i in range(ends)])]
    slice x7 -> x0, local copies, waits for them, and re-layouts: 1.24 us -> none  [the longest x3 1.19 us: with_halo(): head = lax.slice_in_dim(cells, 0, width, axis=dim)]
    mul x5 -> x0, other arithmetic: 0.94 us -> none  [the longest x1 0.73 us: render(): next_trans[None] * colour - remain]
    sub x1 -> x0, other arithmetic: 0.73 us -> none  [body(): data_grad = (1.0 - shares) * feature_grad + carried_in]
    exp x1 -> x0, other arithmetic: 0.62 us -> none  [render(): seg_trans = jnp.exp(-jnp.sum(sigma, axis=1))]
  transfers between devices with their start and end apart: 5 -> 0, of which waited for: 3 -> 0; matrix products, arithmetic and copies ran while one was open for 2% -> 0% of each run, Pallas kernels for 0% -> 0%
where the time goes in v1:
time: 22.5 us; the launch traced here: 22.2 us
  Pallas kernels  17 us (76%)
  local copies, waits for them, and re-layouts  3.21 us (14%)
  other arithmetic  1.36 us (6%)
  between operations  0.67 us (3%)
    pallas_call x1, Pallas kernels, gradient_of_loss(): pl.pallas_call(functools.partial(kernel, tiles, depths, pieces), out_shap...  17 us
    unnamed x12, local copies, waits for them, and re-layouts  3.21 us
    sub x1, other arithmetic, body(): grid - learn_rate * (new_first / corr_one) / (jnp.sqrt(new_second / corr_...  1.36 us

profile of v1, /device:TPU:4, one launch (start us, length us, event | category | flops | bytes accessed | tf_op | source)
XLA Modules:
  0.0 22.2 jit_solution(2208262925809710299)
XLA Ops:
  0.6 0.0 copy-start
  0.6 1.0 %copy-done = f32[4,4,8,1024]{3,2,1,0:T(8,128)S(1)} copy-done((f32[4,4,8,1024]{3,2,1,0:T(8,128)S(1)}, f32[4,4,8,1024]{3,2,1,0:T(8,128)}, u32[]{:S(2)}) %copy-start) | copy-done | bytes 524312
  1.7 0.0 copy-start.1
  1.7 0.8 %copy-done.1 = f32[3,4,1024]{2,1,0:T(4,128)S(1)} copy-done((f32[3,4,1024]{2,1,0:T(4,128)S(1)}, f32[3,4,1024]{2,1,0:T(4,128)}, u32[]{:S(2)}) %copy-start.1) | copy-done | bytes 49176
  2.5 0.0 copy-start.2
  2.5 0.7 %copy-done.2 = s32[4,1024]{1,0:T(4,128)S(1)} copy-done((s32[4,1024]{1,0:T(4,128)S(1)}, s32[4,1024]{1,0:T(4,128)}, u32[]{:S(2)}) %copy-start.2) | copy-done | bytes 16408
  3.2 0.0 copy-start.3
  3.2 0.7 %copy-done.3 = s32[1,1,128]{2,1,0:T(1,128)S(1)} copy-done((s32[1,1,128]{2,1,0:T(1,128)S(1)}, s32[1,1,128]{2,1,0:T(1,128)}, u32[]{:S(2)}) %copy-start.3) | copy-done | bytes 536
  3.8 0.0 copy-start.4
  3.8 0.0 copy-start.5
  3.9 17.0 %shard_map.85 = f32[4,4,8,1024]{3,2,1,0:T(8,128)S(1)} custom-call(f32[4,4,8,1024]{3,2,1,0:T(8,128)S(1)} %copy-done, s32[4,1024]{1,0:T(4,128)S(1)} %copy-done.2, s32[1,1,128]{2,1,0:T(1,128)S(1)} %copy-done.3, f32[3,4,1024]{2,1,0:T(4,128)S(1)} %copy-done.1), custom_call_target="tpu_custom_call" | custom-call | flops 10000000 | bytes 1048576 | tf_op jit(solution)/shard_map/pallas_call | solution.py:381
  20.8 0.0 copy-done.4
  20.8 0.0 copy-done.5
  20.8 1.4 %divide_subtract_fusion = (f32[4,4,8,1024]{3,2,1,0:T(8,128)}, f32[4,4,8,1024]{3,2,1,0:T(8,128)}, f32[4,4,8,1024]{3,2,1,0:T(8,128)}) fusion(f32[4,4,8,1024]{3,2,1,0:T(8,128)S(1)} %copy-done, f32[4,4,8,1024]{3,2,1,0:T(8,128)S(1)} %shard_map.85, f32[4,4,8,1024]{3,2,1,0:T(8,128)S(1)} %copy-done.4, f32[4,4,8,1024]{3,2,1,0:T(8,128)S(1)} %copy-done.5), kind=kLoop, calls=%fused_computation.2 | loop fusion | flops 1572864 | bytes 3670016 | tf_op jit(solution)/shard_map/sub | solution.py:405
Async XLA Ops:
  0.6 1.0 %copy-start = (f32[4,4,8,1024]{3,2,1,0:T(8,128)S(1)}, f32[4,4,8,1024]{3,2,1,0:T(8,128)}, u32[]{:S(2)}) copy-start(f32[4,4,8,1024]{3,2,1,0:T(8,128)} %grid_h.1) | copy-start | bytes 1572868
  1.7 0.8 %copy-start.1 = (f32[3,4,1024]{2,1,0:T(4,128)S(1)}, f32[3,4,1024]{2,1,0:T(4,128)}, u32[]{:S(2)}) copy-start(f32[3,4,1024]{2,1,0:T(4,128)} %tgt_h.1) | copy-start | bytes 147460
  2.5 0.7 %copy-start.2 = (s32[4,1024]{1,0:T(4,128)S(1)}, s32[4,1024]{1,0:T(4,128)}, u32[]{:S(2)}) copy-start(s32[4,1024]{1,0:T(4,128)} %ray_h.1) | copy-start | bytes 49156
  3.2 0.7 %copy-start.3 = (s32[1,1,128]{2,1,0:T(1,128)S(1)}, s32[1,1,128]{2,1,0:T(1,128)}, u32[]{:S(2)}) copy-start(s32[1,1,128]{2,1,0:T(1,128)} %occ_h.1) | copy-start | bytes 1540
  3.8 17.0 %copy-start.4 = (f32[4,4,8,1024]{3,2,1,0:T(8,128)S(1)}, f32[4,4,8,1024]{3,2,1,0:T(8,128)}, u32[]{:S(2)}) copy-start(f32[4,4,8,1024]{3,2,1,0:T(8,128)} %param.7) | copy-start | bytes 1572868
  3.8 17.0 %copy-start.5 = (f32[4,4,8,1024]{3,2,1,0:T(8,128)S(1)}, f32[4,4,8,1024]{3,2,1,0:T(8,128)}, u32[]{:S(2)}) copy-start(f32[4,4,8,1024]{3,2,1,0:T(8,128)} %param.8) | copy-start | bytes 1572868

commit v2 on v1

--- a/solution.py
+++ b/solution.py
@@ -134,11 +134,6 @@
     @pl.when(has_prev)
     def _():
         to_prev.start()
-
-    @pl.when(has_next)
-    def _():
-        to_next.start()
-        ext_next.start()
 
     @pl.when(k < depths - 1)
     def _():
@@ -254,6 +249,25 @@
         put(seg1_out, r, values)
     send_segments(seg1_out, seg1_in, s1_send, s1_recv)
 
+    @pl.when(has_next)
+    def _():
+        to_next.start()
+        ext_next.start()
+
+    lanes = lax.broadcasted_iota(jnp.int32, (planes, width), 1)
+    for c in range(channels):
+        for r in range(rows):
+            here = g[c, r]
+            around = jnp.where(planes_at == 0, 0.0, pltpu.roll(here, 1, 0))
+            around += jnp.where(planes_at == planes - 1, 0.0, pltpu.roll(here, planes - 1, 0))
+            around += jnp.where(lanes == 0, 0.0, pltpu.roll(here, 1, 1))
+            around += jnp.where(lanes == width - 1, 0.0, pltpu.roll(here, width - 1, 1))
+            if r > 0:
+                around += g[c, r - 1]
+            if r < last:
+                around += g[c, r + 1]
+            grad_ref[c, r] = 2.0 * tv_weight * (6.0 * here - around)
+
     pl.when(has_next)(to_prev.wait_recv)
     values = samples(last, lambda c: g[c, last], lambda c: nxt[c, 0], share_of(last), occ)
     put(seg2_out, 0, values)
@@ -265,6 +279,13 @@
 
     when_reduces(k, first_rows)
 
+    @pl.when(has_prev)
+    def _():
+        to_next.wait_recv()
+        ext_next.wait_recv()
+
+    samples(rows, lambda c: prv[c, 0], lambda c: g[c, 0], ext_in[0:1, :], ext_in[1:2, :])
+
     def last_row():
         reduce(seg2_in, qd2_out, s2_send, s2_recv, last, 1)
         send_back(qd2_out, qd2_in, q2_send, q2_recv)
@@ -276,26 +297,15 @@
 
     when_reduces(k, last_row)
 
-    @pl.when(has_prev)
-    def _():
-        to_next.wait_recv()
-        ext_next.wait_recv()
-
-    samples(rows, lambda c: prv[c, 0], lambda c: g[c, 0], ext_in[0:1, :], ext_in[1:2, :])
-
     pl.when(k > 0)(z_back.wait_recv)
     pl.when(k < depths - 1)(z_front.wait_recv)
-    lanes = lax.broadcasted_iota(jnp.int32, (planes, width), 1)
     for c in range(channels):
         for r in range(rows):
-            here = g[c, r]
             i = c * rows + r
-            around = (prv[c, 0] if r == 0 else g[c, r - 1]) + (nxt[c, 0] if r == last else g[c, r + 1])
-            around += jnp.where(planes_at == 0, zin[0, i : i + 1, :], pltpu.roll(here, 1, 0))
-            around += jnp.where(planes_at == planes - 1, zin[1, i : i + 1, :], pltpu.roll(here, planes - 1, 0))
-            around += jnp.where(lanes == 0, 0.0, pltpu.roll(here, 1, 1))
-            around += jnp.where(lanes == width - 1, 0.0, pltpu.roll(here, width - 1, 1))
-            grad_ref[c, r] = 2.0 * tv_weight * (6.0 * here - around)
+            grad_ref[c, r, 0:1, :] -= 2.0 * tv_weight * zin[0, i : i + 1, :]
+            grad_ref[c, r, planes - 1 : planes, :] -= 2.0 * tv_weight * zin[1, i : i + 1, :]
+        grad_ref[c, 0] -= 2.0 * tv_weight * prv[c, 0]
+        grad_ref[c, last] -= 2.0 * tv_weight * nxt[c, 0]
 
     def gradient(slot, qd_in, r):
         q = [jnp.concatenate([qd_in[p, v, r : r + 1, :] for p in range(pieces)], axis=1) for v in range(4)]
@@ -377,7 +387,7 @@
         scratch += [vmem((depths, 4, count, piece), f32), vmem((pieces, 4, count, piece), f32)]
     scratch += [vmem((pieces, 4, 1, piece), f32)]
     scratch += [dma((4,)), dma((5,)), dma((5,))] + [dma((depths,))] * 10
-    hbm = pl.BlockSpec(memory_space=pl.ANY)
+    hbm = pl.BlockSpec(memory_space=pltpu.HBM)
     return pl.pallas_call(
         functools.partial(kernel, tiles, depths, pieces),
         out_shape=jax.ShapeDtypeStruct(grid.shape, f32),
@@ -385,7 +395,7 @@
         out_specs=pl.BlockSpec(memory_space=pltpu.VMEM),
         scratch_shapes=scratch,
         compiler_params=pltpu.CompilerParams(
-            collective_id=0, has_side_effects=True, vmem_limit_bytes=24 * 2**20
+            collective_id=0, has_side_effects=True, vmem_limit_bytes=60 * 2**20
         ),
         cost_estimate=pl.CostEstimate(flops=10**7, bytes_accessed=2**20, transcendentals=10**6),
     )(grid, ray_offset, occupancy, target)

time: 22.5 us -> 20.8 us (0.924)
  local copies, waits for them, and re-layouts: 3.21 us -> 0.01 us
  other arithmetic: 1.36 us -> 2.42 us
  Pallas kernels: 17 us -> 17.5 us
    unnamed x12 -> x6, local copies, waits for them, and re-layouts: 3.21 us -> 0.01 us
    sub x1, other arithmetic: 1.36 us -> 2.42 us  [body(): grid - learn_rate * (new_first / corr_one) / (jnp.sqrt(new_second / corr_...]
    pallas_call x1, Pallas kernels: 17 us -> 17.5 us  [gradient_of_loss(): pl.pallas_call(functools.partial(kernel, tiles, depths, pieces), out_shap...]
where the time goes in v2:
time: 20.8 us; the launch traced here: 20.6 us
  Pallas kernels  17.5 us (84%)
  other arithmetic  2.42 us (12%)
  between operations  0.69 us (3%)
    pallas_call x1, Pallas kernels, gradient_of_loss(): pl.pallas_call(functools.partial(kernel, tiles, depths, pieces), out_shap...  17.5 us
    sub x1, other arithmetic, body(): grid - learn_rate * (new_first / corr_one) / (jnp.sqrt(new_second / corr_...  2.42 us

profile of v2, /device:TPU:4, one launch (start us, length us, event | category | flops | bytes accessed | tf_op | source)
XLA Modules:
  0.0 20.6 jit_solution(15272670751177671918)
XLA Ops:
  0.6 0.0 copy-start
  0.6 0.0 copy-start.2
  0.7 0.0 copy-start.1
  0.7 17.5 %shard_map.85 = f32[4,4,8,1024]{3,2,1,0:T(8,128)} custom-call(f32[4,4,8,1024]{3,2,1,0:T(8,128)} %grid_h.1, s32[4,1024]{1,0:T(4,128)} %ray_h.1, s32[1,1,128]{2,1,0:T(1,128)} %occ_h.1, f32[3,4,1024]{2,1,0:T(4,128)} %tgt_h.1), custom_call_target="tpu_custom_call" | custom-call | flops 10000000 | bytes 1048576 | tf_op jit(solution)/shard_map/pallas_call | solution.py:391
  18.2 0.0 copy-done
  18.2 0.0 copy-done.2
  18.2 0.0 copy-done.1
  18.2 2.4 %divide_subtract_fusion = (f32[4,4,8,1024]{3,2,1,0:T(8,128)}, f32[4,4,8,1024]{3,2,1,0:T(8,128)}, f32[4,4,8,1024]{3,2,1,0:T(8,128)}) fusion(f32[4,4,8,1024]{3,2,1,0:T(8,128)S(1)} %copy-done, f32[4,4,8,1024]{3,2,1,0:T(8,128)} %shard_map.85, f32[4,4,8,1024]{3,2,1,0:T(8,128)S(1)} %copy-done.1, f32[4,4,8,1024]{3,2,1,0:T(8,128)S(1)} %copy-done.2), kind=kLoop, calls=%fused_computation.2 | loop fusion | flops 1572864 | bytes 3670016 | tf_op jit(solution)/shard_map/sub | solution.py:415
Async XLA Ops:
  0.6 17.5 %copy-start = (f32[4,4,8,1024]{3,2,1,0:T(8,128)S(1)}, f32[4,4,8,1024]{3,2,1,0:T(8,128)}, u32[]{:S(2)}) copy-start(f32[4,4,8,1024]{3,2,1,0:T(8,128)} %grid_h.1) | copy-start | bytes 1572868
  0.6 17.5 %copy-start.2 = (f32[4,4,8,1024]{3,2,1,0:T(8,128)S(1)}, f32[4,4,8,1024]{3,2,1,0:T(8,128)}, u32[]{:S(2)}) copy-start(f32[4,4,8,1024]{3,2,1,0:T(8,128)} %param.8) | copy-start | bytes 1572868
  0.7 17.5 %copy-start.1 = (f32[4,4,8,1024]{3,2,1,0:T(8,128)S(1)}, f32[4,4,8,1024]{3,2,1,0:T(8,128)}, u32[]{:S(2)}) copy-start(f32[4,4,8,1024]{3,2,1,0:T(8,128)} %param.7) | copy-start | bytes 1572868

commit v3 on v2

--- a/solution.py
+++ b/solution.py
@@ -97,23 +97,8 @@
     def _():
         zin[1] = jnp.zeros(zin.shape[1:], jnp.float32)
 
-    for load in loads:
-        load.wait()
-
-    blocks = occ_i.shape[2]
-    spread = lax.broadcasted_iota(jnp.int32, (blocks, width), 1) // (width // blocks)
-    spread = (spread == lax.broadcasted_iota(jnp.int32, (blocks, width), 0)).astype(jnp.float32)
-    occ_rows = jnp.broadcast_to(occ_i[0].astype(jnp.float32), (8, blocks))
-    occ = jnp.dot(occ_rows, spread, preferred_element_type=jnp.float32)[0:1]
-    ext_out[0:1, :] = ray[last : last + 1, :].astype(jnp.float32) * 0.5
-    ext_out[1:2, :] = occ
-    for c in range(channels):
-        for r in range(rows):
-            zout[0, c * rows + r : c * rows + r + 1, :] = g[c, r, planes - 1 : planes, :]
-            zout[1, c * rows + r : c * rows + r + 1, :] = g[c, r, 0:1, :]
-
     to_prev = pltpu.make_async_remote_copy(
-        g.at[:, 0:1], nxt, halo_send.at[0], halo_recv.at[0], device_id={"tile": t - 1}, device_id_type=MESH
+        grid_h.at[:, 0:1], nxt, halo_send.at[0], halo_recv.at[0], device_id={"tile": t - 1}, device_id_type=MESH
     )
     to_next = pltpu.make_async_remote_copy(
         g.at[:, last:rows], prv, halo_send.at[1], halo_recv.at[1], device_id={"tile": t + 1}, device_id_type=MESH
@@ -134,6 +119,21 @@
     @pl.when(has_prev)
     def _():
         to_prev.start()
+
+    for load in loads:
+        load.wait()
+
+    blocks = occ_i.shape[2]
+    spread = lax.broadcasted_iota(jnp.int32, (blocks, width), 1) // (width // blocks)
+    spread = (spread == lax.broadcasted_iota(jnp.int32, (blocks, width), 0)).astype(jnp.float32)
+    occ_rows = jnp.broadcast_to(occ_i[0].astype(jnp.float32), (8, blocks))
+    occ = jnp.dot(occ_rows, spread, preferred_element_type=jnp.float32)[0:1]
+    ext_out[0:1, :] = ray[last : last + 1, :].astype(jnp.float32) * 0.5
+    ext_out[1:2, :] = occ
+    for c in range(channels):
+        for r in range(rows):
+            zout[0, c * rows + r : c * rows + r + 1, :] = g[c, r, planes - 1 : planes, :]
+            zout[1, c * rows + r : c * rows + r + 1, :] = g[c, r, 0:1, :]
 
     @pl.when(k < depths - 1)
     def _():
@@ -390,15 +390,15 @@
     hbm = pl.BlockSpec(memory_space=pltpu.HBM)
     return pl.pallas_call(
         functools.partial(kernel, tiles, depths, pieces),
-        out_shape=jax.ShapeDtypeStruct(grid.shape, f32),
+        out_shape=pltpu.VMEM(grid.shape, f32),
         in_specs=[hbm] * 4,
         out_specs=pl.BlockSpec(memory_space=pltpu.VMEM),
         scratch_shapes=scratch,
         compiler_params=pltpu.CompilerParams(
-            collective_id=0, has_side_effects=True, vmem_limit_bytes=60 * 2**20
+            collective_id=0, has_side_effects=True, vmem_limit_bytes=24 * 2**20
         ),
         cost_estimate=pl.CostEstimate(flops=10**7, bytes_accessed=2**20, transcendentals=10**6),
-    )(grid, ray_offset, occupancy, target)
+    )(*(pltpu.with_memory_space_constraint(x, pltpu.HBM) for x in (grid, ray_offset, occupancy, target)))
 
 
 def solution(mesh):

time: 20.8 us -> 19.3 us (0.928)
  other arithmetic: 2.42 us -> 1.38 us
  Pallas kernels: 17.5 us -> 17.1 us
    sub x1, other arithmetic: 2.42 us -> 1.38 us  [body(): grid - learn_rate * (new_first / corr_one) / (jnp.sqrt(new_second / corr_...]
    pallas_call x1, Pallas kernels: 17.5 us -> 17.1 us  [gradient_of_loss(): pl.pallas_call(functools.partial(kernel, tiles, depths, pieces), out_shap...]
where the time goes in v3:
time: 19.3 us; the launch traced here: 19.2 us
  Pallas kernels  17.1 us (89%)
  other arithmetic  1.38 us (7%)
  between operations  0.69 us (4%)
    pallas_call x1, Pallas kernels, gradient_of_loss(): pl.pallas_call(functools.partial(kernel, tiles, depths, pieces), out_shap...  17.1 us
    sub x1, other arithmetic, body(): grid - learn_rate * (new_first / corr_one) / (jnp.sqrt(new_second / corr_...  1.38 us

profile of v3, /device:TPU:4, one launch (start us, length us, event | category | flops | bytes accessed | tf_op | source)
XLA Modules:
  0.0 19.2 jit_solution(5766271077751734779)
XLA Ops:
  0.6 0.0 copy-start
  0.6 0.0 copy-start.2
  0.7 0.0 copy-start.1
  0.7 17.1 %shard_map.85 = f32[4,4,8,1024]{3,2,1,0:T(8,128)S(1)} custom-call(f32[4,4,8,1024]{3,2,1,0:T(8,128)} %grid_h.1, s32[4,1024]{1,0:T(4,128)} %ray_h.1, s32[1,1,128]{2,1,0:T(1,128)} %occ_h.1, f32[3,4,1024]{2,1,0:T(4,128)} %tgt_h.1), custom_call_target="tpu_custom_call" | custom-call | flops 10000000 | bytes 1048576 | tf_op jit(solution)/shard_map/pallas_call | solution.py:391
  17.8 0.0 copy-done
  17.8 0.0 copy-done.2
  17.8 0.0 copy-done.1
  17.8 1.4 %divide_subtract_fusion = (f32[4,4,8,1024]{3,2,1,0:T(8,128)}, f32[4,4,8,1024]{3,2,1,0:T(8,128)}, f32[4,4,8,1024]{3,2,1,0:T(8,128)}) fusion(f32[4,4,8,1024]{3,2,1,0:T(8,128)S(1)} %copy-done, f32[4,4,8,1024]{3,2,1,0:T(8,128)S(1)} %shard_map.85, f32[4,4,8,1024]{3,2,1,0:T(8,128)S(1)} %copy-done.1, f32[4,4,8,1024]{3,2,1,0:T(8,128)S(1)} %copy-done.2), kind=kLoop, calls=%fused_computation.2 | loop fusion | flops 1572864 | bytes 3670016 | tf_op jit(solution)/shard_map/sub | solution.py:415
Async XLA Ops:
  0.6 17.1 %copy-start = (f32[4,4,8,1024]{3,2,1,0:T(8,128)S(1)}, f32[4,4,8,1024]{3,2,1,0:T(8,128)}, u32[]{:S(2)}) copy-start(f32[4,4,8,1024]{3,2,1,0:T(8,128)} %grid_h.1) | copy-start | bytes 1572868
  0.6 17.1 %copy-start.2 = (f32[4,4,8,1024]{3,2,1,0:T(8,128)S(1)}, f32[4,4,8,1024]{3,2,1,0:T(8,128)}, u32[]{:S(2)}) copy-start(f32[4,4,8,1024]{3,2,1,0:T(8,128)} %param.8) | copy-start | bytes 1572868
  0.7 17.1 %copy-start.1 = (f32[4,4,8,1024]{3,2,1,0:T(8,128)S(1)}, f32[4,4,8,1024]{3,2,1,0:T(8,128)}, u32[]{:S(2)}) copy-start(f32[4,4,8,1024]{3,2,1,0:T(8,128)} %param.7) | copy-start | bytes 1572868

commit v4 on v3

--- a/solution.py
+++ b/solution.py
@@ -130,6 +130,11 @@
     occ = jnp.dot(occ_rows, spread, preferred_element_type=jnp.float32)[0:1]
     ext_out[0:1, :] = ray[last : last + 1, :].astype(jnp.float32) * 0.5
     ext_out[1:2, :] = occ
+    @pl.when(has_next)
+    def _():
+        to_next.start()
+        ext_next.start()
+
     for c in range(channels):
         for r in range(rows):
             zout[0, c * rows + r : c * rows + r + 1, :] = g[c, r, planes - 1 : planes, :]
@@ -249,10 +254,16 @@
         put(seg1_out, r, values)
     send_segments(seg1_out, seg1_in, s1_send, s1_recv)
 
-    @pl.when(has_next)
-    def _():
-        to_next.start()
-        ext_next.start()
+    pl.when(has_next)(to_prev.wait_recv)
+    values = samples(last, lambda c: g[c, last], lambda c: nxt[c, 0], share_of(last), occ)
+    put(seg2_out, 0, values)
+    send_segments(seg2_out, seg2_in, s2_send, s2_recv)
+
+    def first_rows():
+        reduce(seg1_in, qd1_out, s1_send, s1_recv, 0, last)
+        send_back(qd1_out, qd1_in, q1_send, q1_recv)
+
+    when_reduces(k, first_rows)
 
     lanes = lax.broadcasted_iota(jnp.int32, (planes, width), 1)
     for c in range(channels):
@@ -268,24 +279,6 @@
                 around += g[c, r + 1]
             grad_ref[c, r] = 2.0 * tv_weight * (6.0 * here - around)
 
-    pl.when(has_next)(to_prev.wait_recv)
-    values = samples(last, lambda c: g[c, last], lambda c: nxt[c, 0], share_of(last), occ)
-    put(seg2_out, 0, values)
-    send_segments(seg2_out, seg2_in, s2_send, s2_recv)
-
-    def first_rows():
-        reduce(seg1_in, qd1_out, s1_send, s1_recv, 0, last)
-        send_back(qd1_out, qd1_in, q1_send, q1_recv)
-
-    when_reduces(k, first_rows)
-
-    @pl.when(has_prev)
-    def _():
-        to_next.wait_recv()
-        ext_next.wait_recv()
-
-    samples(rows, lambda c: prv[c, 0], lambda c: g[c, 0], ext_in[0:1, :], ext_in[1:2, :])
-
     def last_row():
         reduce(seg2_in, qd2_out, s2_send, s2_recv, last, 1)
         send_back(qd2_out, qd2_in, q2_send, q2_recv)
@@ -296,6 +289,13 @@
                 qd_copy_next(d).start()
 
     when_reduces(k, last_row)
+
+    @pl.when(has_prev)
+    def _():
+        to_next.wait_recv()
+        ext_next.wait_recv()
+
+    samples(rows, lambda c: prv[c, 0], lambda c: g[c, 0], ext_in[0:1, :], ext_in[1:2, :])
 
     pl.when(k > 0)(z_back.wait_recv)
     pl.when(k < depths - 1)(z_front.wait_recv)

time: 19.3 us -> 19.3 us (level)
  no operation moved by 1% of the time
where the time goes in v4:
time: 19.3 us; the launch traced here: 19.2 us
  Pallas kernels  17.1 us (89%)
  other arithmetic  1.38 us (7%)
  between operations  0.69 us (4%)
    pallas_call x1, Pallas kernels, gradient_of_loss(): pl.pallas_call(functools.partial(kernel, tiles, depths, pieces), out_shap...  17.1 us
    sub x1, other arithmetic, body(): grid - learn_rate * (new_first / corr_one) / (jnp.sqrt(new_second / corr_...  1.38 us

profile of v4, /device:TPU:4, one launch (start us, length us, event | category | flops | bytes accessed | tf_op | source)
XLA Modules:
  0.0 19.2 jit_solution(5264980341036893892)
XLA Ops:
  0.6 0.0 copy-start
  0.6 0.0 copy-start.2
  0.7 0.0 copy-start.1
  0.7 17.1 %shard_map.85 = f32[4,4,8,1024]{3,2,1,0:T(8,128)S(1)} custom-call(f32[4,4,8,1024]{3,2,1,0:T(8,128)} %grid_h.1, s32[4,1024]{1,0:T(4,128)} %ray_h.1, s32[1,1,128]{2,1,0:T(1,128)} %occ_h.1, f32[3,4,1024]{2,1,0:T(4,128)} %tgt_h.1), custom_call_target="tpu_custom_call" | custom-call | flops 10000000 | bytes 1048576 | tf_op jit(solution)/shard_map/pallas_call | solution.py:391
  17.8 0.0 copy-done
  17.8 0.0 copy-done.2
  17.8 0.0 copy-done.1
  17.8 1.4 %divide_subtract_fusion = (f32[4,4,8,1024]{3,2,1,0:T(8,128)}, f32[4,4,8,1024]{3,2,1,0:T(8,128)}, f32[4,4,8,1024]{3,2,1,0:T(8,128)}) fusion(f32[4,4,8,1024]{3,2,1,0:T(8,128)S(1)} %copy-done, f32[4,4,8,1024]{3,2,1,0:T(8,128)S(1)} %shard_map.85, f32[4,4,8,1024]{3,2,1,0:T(8,128)S(1)} %copy-done.1, f32[4,4,8,1024]{3,2,1,0:T(8,128)S(1)} %copy-done.2), kind=kLoop, calls=%fused_computation.2 | loop fusion | flops 1572864 | bytes 3670016 | tf_op jit(solution)/shard_map/sub | solution.py:415
Async XLA Ops:
  0.6 17.1 %copy-start = (f32[4,4,8,1024]{3,2,1,0:T(8,128)S(1)}, f32[4,4,8,1024]{3,2,1,0:T(8,128)}, u32[]{:S(2)}) copy-start(f32[4,4,8,1024]{3,2,1,0:T(8,128)} %grid_h.1) | copy-start | bytes 1572868
  0.6 17.1 %copy-start.2 = (f32[4,4,8,1024]{3,2,1,0:T(8,128)S(1)}, f32[4,4,8,1024]{3,2,1,0:T(8,128)}, u32[]{:S(2)}) copy-start(f32[4,4,8,1024]{3,2,1,0:T(8,128)} %param.8) | copy-start | bytes 1572868
  0.7 17.1 %copy-start.1 = (f32[4,4,8,1024]{3,2,1,0:T(8,128)S(1)}, f32[4,4,8,1024]{3,2,1,0:T(8,128)}, u32[]{:S(2)}) copy-start(f32[4,4,8,1024]{3,2,1,0:T(8,128)} %param.7) | copy-start | bytes 1572868

commit v5 on v4

--- a/solution.py
+++ b/solution.py
@@ -45,10 +45,10 @@
     g, ray, occ_i, tgt, nxt, prv, ext_out, ext_in, zout, zin,
     col, wgt, ntr, dfac,
     seg1_out, seg1_in, seg2_out, seg2_in,
-    qd1_out, qd1_in, qd2_out, qd2_in, qdp_in,
+    qd1_out, qd1_in, qd2_out, qd2_in,
     load_sem, halo_send, halo_recv,
     s1_send, s1_recv, s2_send, s2_recv,
-    q1_send, q1_recv, q2_send, q2_recv, qp_send, qp_recv,
+    q1_send, q1_recv, q2_send, q2_recv,
 ):
     t, k = lax.axis_index("tile"), lax.axis_index("depth")
     channels, rows, planes, width = g.shape
@@ -71,19 +71,16 @@
 
     @pl.when(has_prev)
     def _():
-        for j in range(depths):
-            pl.semaphore_signal(barrier, inc=1, device_id={"tile": t - 1, "depth": j}, device_id_type=MESH)
+        pl.semaphore_signal(barrier, inc=1, device_id={"tile": t - 1}, device_id_type=MESH)
 
     @pl.when(has_next)
     def _():
-        for j in range(depths):
-            pl.semaphore_signal(barrier, inc=1, device_id={"tile": t + 1, "depth": j}, device_id_type=MESH)
+        pl.semaphore_signal(barrier, inc=1, device_id={"tile": t + 1}, device_id_type=MESH)
 
     @pl.when(jnp.logical_not(has_prev))
     def _():
         prv[...] = jnp.zeros_like(prv)
         ext_in[...] = jnp.zeros_like(ext_in)
-        qdp_in[...] = jnp.zeros_like(qdp_in)
 
     @pl.when(jnp.logical_not(has_next))
     def _():
@@ -101,7 +98,7 @@
         grid_h.at[:, 0:1], nxt, halo_send.at[0], halo_recv.at[0], device_id={"tile": t - 1}, device_id_type=MESH
     )
     to_next = pltpu.make_async_remote_copy(
-        g.at[:, last:rows], prv, halo_send.at[1], halo_recv.at[1], device_id={"tile": t + 1}, device_id_type=MESH
+        grid_h.at[:, last:rows], prv, halo_send.at[1], halo_recv.at[1], device_id={"tile": t + 1}, device_id_type=MESH
     )
     ext_next = pltpu.make_async_remote_copy(
         ext_out, ext_in, halo_send.at[2], halo_recv.at[2], device_id={"tile": t + 1}, device_id_type=MESH
@@ -113,12 +110,16 @@
         zout.at[1], zin.at[1], halo_send.at[4], halo_recv.at[4], device_id={"depth": k - 1}, device_id_type=MESH
     )
 
-    partners = depths - 1 + depths * (has_prev.astype(jnp.int32) + has_next.astype(jnp.int32))
+    partners = depths - 1 + has_prev.astype(jnp.int32) + has_next.astype(jnp.int32)
     pl.semaphore_wait(barrier, partners)
 
     @pl.when(has_prev)
     def _():
         to_prev.start()
+
+    @pl.when(has_next)
+    def _():
+        to_next.start()
 
     for load in loads:
         load.wait()
@@ -130,9 +131,10 @@
     occ = jnp.dot(occ_rows, spread, preferred_element_type=jnp.float32)[0:1]
     ext_out[0:1, :] = ray[last : last + 1, :].astype(jnp.float32) * 0.5
     ext_out[1:2, :] = occ
+    for c in range(3):
+        ext_out[2 + c : 3 + c, :] = tgt[c, last : last + 1, :]
     @pl.when(has_next)
     def _():
-        to_next.start()
         ext_next.start()
 
     for c in range(channels):
@@ -199,7 +201,7 @@
 
         when_reduces(k, own)
 
-    def reduce(seg_in, qd_out, send, recv, first, count):
+    def reduce(seg_in, qd_out, send, recv, wanted):
         for d in range(1, depths):
             source = lax.rem(k + d, depths)
             seg_copy(seg_in, seg_in, send, recv, d, source).wait_recv()
@@ -214,7 +216,7 @@
             front = front * seg_in[j, 3]
             fronts.append(front)
         half = 0.5 * planes * depths
-        pg = [half * (pixel[c] + front - tgt[c, first : first + count, at]) for c in range(3)]
+        pg = [half * (pixel[c] + front - wanted(c, at)) for c in range(3)]
         behind = pg[0] + pg[1] + pg[2]
         for j in range(depths - 1, -1, -1):
             for c in range(3):
@@ -231,14 +233,6 @@
             device_id={"depth": to}, device_id_type=MESH,
         )
 
-    def qd_copy_next(d, source=None):
-        to = lax.rem(k + d, depths)
-        slot = k % pieces if source is None else source % pieces
-        return pltpu.make_async_remote_copy(
-            qd2_out.at[to], qdp_in.at[slot], qp_send.at[d], qp_recv.at[slot],
-            device_id={"tile": t + 1, "depth": to}, device_id_type=MESH,
-        )
-
     def send_back(qd_out, qd_in, send, recv):
         for d in range(1, depths):
             qd_copy(qd_out, qd_in, send, recv, d).start()
@@ -257,10 +251,18 @@
     pl.when(has_next)(to_prev.wait_recv)
     values = samples(last, lambda c: g[c, last], lambda c: nxt[c, 0], share_of(last), occ)
     put(seg2_out, 0, values)
+
+    @pl.when(has_prev)
+    def _():
+        to_next.wait_recv()
+        ext_next.wait_recv()
+
+    values = samples(rows, lambda c: prv[c, 0], lambda c: g[c, 0], ext_in[0:1, :], ext_in[1:2, :])
+    put(seg2_out, 1, values)
     send_segments(seg2_out, seg2_in, s2_send, s2_recv)
 
     def first_rows():
-        reduce(seg1_in, qd1_out, s1_send, s1_recv, 0, last)
+        reduce(seg1_in, qd1_out, s1_send, s1_recv, lambda c, at: tgt[c, 0:last, at])
         send_back(qd1_out, qd1_in, q1_send, q1_recv)
 
     when_reduces(k, first_rows)
@@ -280,22 +282,13 @@
             grad_ref[c, r] = 2.0 * tv_weight * (6.0 * here - around)
 
     def last_row():
-        reduce(seg2_in, qd2_out, s2_send, s2_recv, last, 1)
+        reduce(
+            seg2_in, qd2_out, s2_send, s2_recv,
+            lambda c, at: jnp.concatenate([tgt[c, last:rows, at], ext_in[2 + c : 3 + c, at]], axis=0),
+        )
         send_back(qd2_out, qd2_in, q2_send, q2_recv)
 
-        @pl.when(has_next)
-        def _():
-            for d in range(depths):
-                qd_copy_next(d).start()
-
     when_reduces(k, last_row)
-
-    @pl.when(has_prev)
-    def _():
-        to_next.wait_recv()
-        ext_next.wait_recv()
-
-    samples(rows, lambda c: prv[c, 0], lambda c: g[c, 0], ext_in[0:1, :], ext_in[1:2, :])
 
     pl.when(k > 0)(z_back.wait_recv)
     pl.when(k < depths - 1)(z_front.wait_recv)
@@ -331,13 +324,7 @@
     wait_back(qd2_in, q2_send, q2_recv)
     add(last, 1.0 - share_of(last), gradient(last, qd2_in, 0))
 
-    @pl.when(has_prev)
-    def _():
-        for d in range(depths):
-            source = lax.rem(k + d, depths)
-            when_reduces(source, qd_copy_next(d, source).wait_recv)
-
-    add(0, ext_in[0:1, :], gradient(rows, qdp_in, 0))
+    add(0, ext_in[0:1, :], gradient(rows, qd2_in, 1))
 
     pl.when(has_prev)(to_prev.wait_send)
 
@@ -357,11 +344,6 @@
         for d in range(1, depths):
             qd_copy(qd1_out, qd1_in, q1_send, q1_recv, d).wait_send()
             qd_copy(qd2_out, qd2_in, q2_send, q2_recv, d).wait_send()
-
-        @pl.when(has_next)
-        def _():
-            for d in range(depths):
-                qd_copy_next(d).wait_send()
 
     when_reduces(k, sent_back)
 
@@ -381,12 +363,11 @@
         vmem((rows + 1, 3, planes, width), f32), vmem((rows + 1, planes, width), f32),
         vmem((rows + 1, planes, width), f32), vmem((rows + 1, planes, width), f32),
     ]
-    for count in (rows - 1, 1):
+    for count in (rows - 1, 2):
         scratch += [vmem((pieces, 4, count, piece), f32), vmem((depths, 4, count, piece), f32)]
-    for count in (rows - 1, 1):
+    for count in (rows - 1, 2):
         scratch += [vmem((depths, 4, count, piece), f32), vmem((pieces, 4, count, piece), f32)]
-    scratch += [vmem((pieces, 4, 1, piece), f32)]
-    scratch += [dma((4,)), dma((5,)), dma((5,))] + [dma((depths,))] * 10
+    scratch += [dma((4,)), dma((5,)), dma((5,))] + [dma((depths,))] * 8
     hbm = pl.BlockSpec(memory_space=pltpu.HBM)
     return pl.pallas_call(
         functools.partial(kernel, tiles, depths, pieces),

time: 19.3 us -> 19.1 us (0.990)
  the two profiles are of different devices: /device:TPU:4 before, /device:TPU:1 now
where the time goes in v5:
time: 19.1 us; the launch traced here: 18.9 us
  Pallas kernels  16.8 us (88%)
  other arithmetic  1.38 us (7%)
  between operations  0.69 us (4%)
    pallas_call x1, Pallas kernels, gradient_of_loss(): pl.pallas_call(functools.partial(kernel, tiles, depths, pieces), out_shap...  16.8 us
    sub x1, other arithmetic, body(): grid - learn_rate * (new_first / corr_one) / (jnp.sqrt(new_second / corr_...  1.38 us

profile of v5, /device:TPU:1, one launch (start us, length us, event | category | flops | bytes accessed | tf_op | source)
XLA Modules:
  0.0 18.9 jit_solution(11684032366540137113)
XLA Ops:
  0.6 0.0 copy-start
  0.6 0.0 copy-start.2
  0.7 0.0 copy-start.1
  0.7 16.8 %shard_map.85 = f32[4,4,8,1024]{3,2,1,0:T(8,128)S(1)} custom-call(f32[4,4,8,1024]{3,2,1,0:T(8,128)} %grid_h.1, s32[4,1024]{1,0:T(4,128)} %ray_h.1, s32[1,1,128]{2,1,0:T(1,128)} %occ_h.1, f32[3,4,1024]{2,1,0:T(4,128)} %tgt_h.1), custom_call_target="tpu_custom_call" | custom-call | flops 10000000 | bytes 1048576 | tf_op jit(solution)/shard_map/pallas_call | solution.py:372
  17.5 0.0 copy-done
  17.5 0.0 copy-done.2
  17.5 0.0 copy-done.1
  17.5 1.4 %divide_subtract_fusion = (f32[4,4,8,1024]{3,2,1,0:T(8,128)}, f32[4,4,8,1024]{3,2,1,0:T(8,128)}, f32[4,4,8,1024]{3,2,1,0:T(8,128)}) fusion(f32[4,4,8,1024]{3,2,1,0:T(8,128)S(1)} %copy-done, f32[4,4,8,1024]{3,2,1,0:T(8,128)S(1)} %shard_map.85, f32[4,4,8,1024]{3,2,1,0:T(8,128)S(1)} %copy-done.1, f32[4,4,8,1024]{3,2,1,0:T(8,128)S(1)} %copy-done.2), kind=kLoop, calls=%fused_computation.2 | loop fusion | flops 1572864 | bytes 3670016 | tf_op jit(solution)/shard_map/sub | solution.py:396
Async XLA Ops:
  0.6 16.9 %copy-start = (f32[4,4,8,1024]{3,2,1,0:T(8,128)S(1)}, f32[4,4,8,1024]{3,2,1,0:T(8,128)}, u32[]{:S(2)}) copy-start(f32[4,4,8,1024]{3,2,1,0:T(8,128)} %grid_h.1) | copy-start | bytes 1572868
  0.6 16.9 %copy-start.2 = (f32[4,4,8,1024]{3,2,1,0:T(8,128)S(1)}, f32[4,4,8,1024]{3,2,1,0:T(8,128)}, u32[]{:S(2)}) copy-start(f32[4,4,8,1024]{3,2,1,0:T(8,128)} %param.8) | copy-start | bytes 1572868
  0.7 16.9 %copy-start.1 = (f32[4,4,8,1024]{3,2,1,0:T(8,128)S(1)}, f32[4,4,8,1024]{3,2,1,0:T(8,128)}, u32[]{:S(2)}) copy-start(f32[4,4,8,1024]{3,2,1,0:T(8,128)} %param.7) | copy-start | bytes 1572868

commit v6 on v4

--- a/solution.py
+++ b/solution.py
@@ -130,11 +130,6 @@
     occ = jnp.dot(occ_rows, spread, preferred_element_type=jnp.float32)[0:1]
     ext_out[0:1, :] = ray[last : last + 1, :].astype(jnp.float32) * 0.5
     ext_out[1:2, :] = occ
-    @pl.when(has_next)
-    def _():
-        to_next.start()
-        ext_next.start()
-
     for c in range(channels):
         for r in range(rows):
             zout[0, c * rows + r : c * rows + r + 1, :] = g[c, r, planes - 1 : planes, :]
@@ -254,7 +249,12 @@
         put(seg1_out, r, values)
     send_segments(seg1_out, seg1_in, s1_send, s1_recv)
 
-    pl.when(has_next)(to_prev.wait_recv)
+    @pl.when(has_next)
+    def _():
+        to_prev.wait_recv()
+        to_next.start()
+        ext_next.start()
+
     values = samples(last, lambda c: g[c, last], lambda c: nxt[c, 0], share_of(last), occ)
     put(seg2_out, 0, values)
     send_segments(seg2_out, seg2_in, s2_send, s2_recv)
@@ -281,12 +281,13 @@
 
     def last_row():
         reduce(seg2_in, qd2_out, s2_send, s2_recv, last, 1)
-        send_back(qd2_out, qd2_in, q2_send, q2_recv)
 
         @pl.when(has_next)
         def _():
             for d in range(depths):
                 qd_copy_next(d).start()
+
+        send_back(qd2_out, qd2_in, q2_send, q2_recv)
 
     when_reduces(k, last_row)
 

time: 19.3 us -> 18.2 us (0.943)
  Pallas kernels: 17.1 us -> 16 us
    pallas_call x1, Pallas kernels: 17.1 us -> 16 us  [gradient_of_loss(): pl.pallas_call(functools.partial(kernel, tiles, depths, pieces), out_shap...]
where the time goes in v6:
time: 18.2 us; the launch traced here: 18 us
  Pallas kernels  16 us (88%)
  other arithmetic  1.38 us (8%)
  between operations  0.69 us (4%)
    pallas_call x1, Pallas kernels, gradient_of_loss(): pl.pallas_call(functools.partial(kernel, tiles, depths, pieces), out_shap...  16 us
    sub x1, other arithmetic, body(): grid - learn_rate * (new_first / corr_one) / (jnp.sqrt(new_second / corr_...  1.38 us

profile of v6, /device:TPU:4, one launch (start us, length us, event | category | flops | bytes accessed | tf_op | source)
XLA Modules:
  0.0 18.0 jit_solution(14097129302742087432)
XLA Ops:
  0.6 0.0 copy-start
  0.6 0.0 copy-start.2
  0.7 0.0 copy-start.1
  0.7 16.0 %shard_map.85 = f32[4,4,8,1024]{3,2,1,0:T(8,128)S(1)} custom-call(f32[4,4,8,1024]{3,2,1,0:T(8,128)} %grid_h.1, s32[4,1024]{1,0:T(4,128)} %ray_h.1, s32[1,1,128]{2,1,0:T(1,128)} %occ_h.1, f32[3,4,1024]{2,1,0:T(4,128)} %tgt_h.1), custom_call_target="tpu_custom_call" | custom-call | flops 10000000 | bytes 1048576 | tf_op jit(solution)/shard_map/pallas_call | solution.py:392
  16.6 0.0 copy-done
  16.6 0.0 copy-done.2
  16.7 0.0 copy-done.1
  16.7 1.4 %divide_subtract_fusion = (f32[4,4,8,1024]{3,2,1,0:T(8,128)}, f32[4,4,8,1024]{3,2,1,0:T(8,128)}, f32[4,4,8,1024]{3,2,1,0:T(8,128)}) fusion(f32[4,4,8,1024]{3,2,1,0:T(8,128)S(1)} %copy-done, f32[4,4,8,1024]{3,2,1,0:T(8,128)S(1)} %shard_map.85, f32[4,4,8,1024]{3,2,1,0:T(8,128)S(1)} %copy-done.1, f32[4,4,8,1024]{3,2,1,0:T(8,128)S(1)} %copy-done.2), kind=kLoop, calls=%fused_computation.2 | loop fusion | flops 1572864 | bytes 3670016 | tf_op jit(solution)/shard_map/sub | solution.py:416
Async XLA Ops:
  0.6 16.0 %copy-start = (f32[4,4,8,1024]{3,2,1,0:T(8,128)S(1)}, f32[4,4,8,1024]{3,2,1,0:T(8,128)}, u32[]{:S(2)}) copy-start(f32[4,4,8,1024]{3,2,1,0:T(8,128)} %grid_h.1) | copy-start | bytes 1572868
  0.6 16.0 %copy-start.2 = (f32[4,4,8,1024]{3,2,1,0:T(8,128)S(1)}, f32[4,4,8,1024]{3,2,1,0:T(8,128)}, u32[]{:S(2)}) copy-start(f32[4,4,8,1024]{3,2,1,0:T(8,128)} %param.8) | copy-start | bytes 1572868
  0.7 16.0 %copy-start.1 = (f32[4,4,8,1024]{3,2,1,0:T(8,128)S(1)}, f32[4,4,8,1024]{3,2,1,0:T(8,128)}, u32[]{:S(2)}) copy-start(f32[4,4,8,1024]{3,2,1,0:T(8,128)} %param.7) | copy-start | bytes 1572868

commit v7 on v3

--- a/solution.py
+++ b/solution.py
@@ -244,18 +244,9 @@
             source = lax.rem(k + d, depths)
             when_reduces(source, qd_copy(qd_in, qd_in, send, recv, d, source).wait_recv)
 
-    for r in range(last):
-        values = samples(r, lambda c: g[c, r], lambda c: g[c, r + 1], share_of(r), occ)
-        put(seg1_out, r, values)
-    send_segments(seg1_out, seg1_in, s1_send, s1_recv)
-
-    @pl.when(has_next)
-    def _():
-        to_next.start()
-        ext_next.start()
-
     lanes = lax.broadcasted_iota(jnp.int32, (planes, width), 1)
-    for c in range(channels):
+
+    def smooth_within(c):
         for r in range(rows):
             here = g[c, r]
             around = jnp.where(planes_at == 0, 0.0, pltpu.roll(here, 1, 0))
@@ -268,7 +259,20 @@
                 around += g[c, r + 1]
             grad_ref[c, r] = 2.0 * tv_weight * (6.0 * here - around)
 
-    pl.when(has_next)(to_prev.wait_recv)
+    for r in range(last):
+        values = samples(r, lambda c: g[c, r], lambda c: g[c, r + 1], share_of(r), occ)
+        put(seg1_out, r, values)
+    send_segments(seg1_out, seg1_in, s1_send, s1_recv)
+
+    for c in range(channels // 2):
+        smooth_within(c)
+
+    @pl.when(has_next)
+    def _():
+        to_prev.wait_recv()
+        to_next.start()
+        ext_next.start()
+
     values = samples(last, lambda c: g[c, last], lambda c: nxt[c, 0], share_of(last), occ)
     put(seg2_out, 0, values)
     send_segments(seg2_out, seg2_in, s2_send, s2_recv)
@@ -279,21 +283,18 @@
 
     when_reduces(k, first_rows)
 
-    @pl.when(has_prev)
-    def _():
-        to_next.wait_recv()
-        ext_next.wait_recv()
-
-    samples(rows, lambda c: prv[c, 0], lambda c: g[c, 0], ext_in[0:1, :], ext_in[1:2, :])
+    for c in range(channels // 2, channels):
+        smooth_within(c)
 
     def last_row():
         reduce(seg2_in, qd2_out, s2_send, s2_recv, last, 1)
-        send_back(qd2_out, qd2_in, q2_send, q2_recv)
 
         @pl.when(has_next)
         def _():
             for d in range(depths):
                 qd_copy_next(d).start()
+
+        send_back(qd2_out, qd2_in, q2_send, q2_recv)
 
     when_reduces(k, last_row)
 
@@ -304,7 +305,6 @@
             i = c * rows + r
             grad_ref[c, r, 0:1, :] -= 2.0 * tv_weight * zin[0, i : i + 1, :]
             grad_ref[c, r, planes - 1 : planes, :] -= 2.0 * tv_weight * zin[1, i : i + 1, :]
-        grad_ref[c, 0] -= 2.0 * tv_weight * prv[c, 0]
         grad_ref[c, last] -= 2.0 * tv_weight * nxt[c, 0]
 
     def gradient(slot, qd_in, r):
@@ -328,6 +328,15 @@
         values = gradient(r, qd1_in, r)
         add(r, 1.0 - share_of(r), values)
         add(r + 1, share_of(r), values)
+    @pl.when(has_prev)
+    def _():
+        to_next.wait_recv()
+        ext_next.wait_recv()
+
+    samples(rows, lambda c: prv[c, 0], lambda c: g[c, 0], ext_in[0:1, :], ext_in[1:2, :])
+    for c in range(channels):
+        grad_ref[c, 0] -= 2.0 * tv_weight * prv[c, 0]
+
     wait_back(qd2_in, q2_send, q2_recv)
     add(last, 1.0 - share_of(last), gradient(last, qd2_in, 0))
 

time: 19.3 us -> 18.2 us (0.943)
  Pallas kernels: 17.1 us -> 16 us
    pallas_call x1, Pallas kernels: 17.1 us -> 16 us  [gradient_of_loss(): pl.pallas_call(functools.partial(kernel, tiles, depths, pieces), out_shap...]
where the time goes in v7:
time: 18.2 us; the launch traced here: 18 us
  Pallas kernels  16 us (88%)
  other arithmetic  1.38 us (8%)
  between operations  0.69 us (4%)
    pallas_call x1, Pallas kernels, gradient_of_loss(): pl.pallas_call(functools.partial(kernel, tiles, depths, pieces), out_shap...  16 us
    sub x1, other arithmetic, body(): grid - learn_rate * (new_first / corr_one) / (jnp.sqrt(new_second / corr_...  1.38 us

profile of v7, /device:TPU:4, one launch (start us, length us, event | category | flops | bytes accessed | tf_op | source)
XLA Modules:
  0.0 18.0 jit_solution(14038976669148570010)
XLA Ops:
  0.6 0.0 copy-start
  0.6 0.0 copy-start.2
  0.7 0.0 copy-start.1
  0.7 16.0 %shard_map.85 = f32[4,4,8,1024]{3,2,1,0:T(8,128)S(1)} custom-call(f32[4,4,8,1024]{3,2,1,0:T(8,128)} %grid_h.1, s32[4,1024]{1,0:T(4,128)} %ray_h.1, s32[1,1,128]{2,1,0:T(1,128)} %occ_h.1, f32[3,4,1024]{2,1,0:T(4,128)} %tgt_h.1), custom_call_target="tpu_custom_call" | custom-call | flops 10000000 | bytes 1048576 | tf_op jit(solution)/shard_map/pallas_call | solution.py:400
  16.6 0.0 copy-done
  16.6 0.0 copy-done.2
  16.7 0.0 copy-done.1
  16.7 1.4 %divide_subtract_fusion = (f32[4,4,8,1024]{3,2,1,0:T(8,128)}, f32[4,4,8,1024]{3,2,1,0:T(8,128)}, f32[4,4,8,1024]{3,2,1,0:T(8,128)}) fusion(f32[4,4,8,1024]{3,2,1,0:T(8,128)S(1)} %copy-done, f32[4,4,8,1024]{3,2,1,0:T(8,128)S(1)} %shard_map.85, f32[4,4,8,1024]{3,2,1,0:T(8,128)S(1)} %copy-done.1, f32[4,4,8,1024]{3,2,1,0:T(8,128)S(1)} %copy-done.2), kind=kLoop, calls=%fused_computation.2 | loop fusion | flops 1572864 | bytes 3670016 | tf_op jit(solution)/shard_map/sub | solution.py:424
Async XLA Ops:
  0.6 16.0 %copy-start = (f32[4,4,8,1024]{3,2,1,0:T(8,128)S(1)}, f32[4,4,8,1024]{3,2,1,0:T(8,128)}, u32[]{:S(2)}) copy-start(f32[4,4,8,1024]{3,2,1,0:T(8,128)} %grid_h.1) | copy-start | bytes 1572868
  0.6 16.0 %copy-start.2 = (f32[4,4,8,1024]{3,2,1,0:T(8,128)S(1)}, f32[4,4,8,1024]{3,2,1,0:T(8,128)}, u32[]{:S(2)}) copy-start(f32[4,4,8,1024]{3,2,1,0:T(8,128)} %param.8) | copy-start | bytes 1572868
  0.7 16.0 %copy-start.1 = (f32[4,4,8,1024]{3,2,1,0:T(8,128)S(1)}, f32[4,4,8,1024]{3,2,1,0:T(8,128)}, u32[]{:S(2)}) copy-start(f32[4,4,8,1024]{3,2,1,0:T(8,128)} %param.7) | copy-start | bytes 1572868

commit v8 on v7

--- a/solution.py
+++ b/solution.py
@@ -281,8 +281,6 @@
         reduce(seg1_in, qd1_out, s1_send, s1_recv, 0, last)
         send_back(qd1_out, qd1_in, q1_send, q1_recv)
 
-    when_reduces(k, first_rows)
-
     for c in range(channels // 2, channels):
         smooth_within(c)
 
@@ -297,6 +295,8 @@
         send_back(qd2_out, qd2_in, q2_send, q2_recv)
 
     when_reduces(k, last_row)
+
+    when_reduces(k, first_rows)
 
     pl.when(k > 0)(z_back.wait_recv)
     pl.when(k < depths - 1)(z_front.wait_recv)

time: 18.2 us -> 18.4 us (1.011)
  no operation moved by 1% of the time
where the time goes in v8:
time: 18.4 us; the launch traced here: 18.1 us
  Pallas kernels  16 us (87%)
  other arithmetic  1.38 us (8%)
  between operations  0.69 us (4%)
    pallas_call x1, Pallas kernels, gradient_of_loss(): pl.pallas_call(functools.partial(kernel, tiles, depths, pieces), out_shap...  16 us
    sub x1, other arithmetic, body(): grid - learn_rate * (new_first / corr_one) / (jnp.sqrt(new_second / corr_...  1.38 us

profile of v8, /device:TPU:4, one launch (start us, length us, event | category | flops | bytes accessed | tf_op | source)
XLA Modules:
  0.0 18.1 jit_solution(13559899217103785733)
XLA Ops:
  0.6 0.0 copy-start
  0.6 0.0 copy-start.2
  0.7 0.0 copy-start.1
  0.7 16.0 %shard_map.85 = f32[4,4,8,1024]{3,2,1,0:T(8,128)S(1)} custom-call(f32[4,4,8,1024]{3,2,1,0:T(8,128)} %grid_h.1, s32[4,1024]{1,0:T(4,128)} %ray_h.1, s32[1,1,128]{2,1,0:T(1,128)} %occ_h.1, f32[3,4,1024]{2,1,0:T(4,128)} %tgt_h.1), custom_call_target="tpu_custom_call" | custom-call | flops 10000000 | bytes 1048576 | tf_op jit(solution)/shard_map/pallas_call | solution.py:400
  16.7 0.0 copy-done
  16.7 0.0 copy-done.2
  16.7 0.0 copy-done.1
  16.7 1.4 %divide_subtract_fusion = (f32[4,4,8,1024]{3,2,1,0:T(8,128)}, f32[4,4,8,1024]{3,2,1,0:T(8,128)}, f32[4,4,8,1024]{3,2,1,0:T(8,128)}) fusion(f32[4,4,8,1024]{3,2,1,0:T(8,128)S(1)} %copy-done, f32[4,4,8,1024]{3,2,1,0:T(8,128)S(1)} %shard_map.85, f32[4,4,8,1024]{3,2,1,0:T(8,128)S(1)} %copy-done.1, f32[4,4,8,1024]{3,2,1,0:T(8,128)S(1)} %copy-done.2), kind=kLoop, calls=%fused_computation.2 | loop fusion | flops 1572864 | bytes 3670016 | tf_op jit(solution)/shard_map/sub | solution.py:424
Async XLA Ops:
  0.6 16.1 %copy-start = (f32[4,4,8,1024]{3,2,1,0:T(8,128)S(1)}, f32[4,4,8,1024]{3,2,1,0:T(8,128)}, u32[]{:S(2)}) copy-start(f32[4,4,8,1024]{3,2,1,0:T(8,128)} %grid_h.1) | copy-start | bytes 1572868
  0.6 16.1 %copy-start.2 = (f32[4,4,8,1024]{3,2,1,0:T(8,128)S(1)}, f32[4,4,8,1024]{3,2,1,0:T(8,128)}, u32[]{:S(2)}) copy-start(f32[4,4,8,1024]{3,2,1,0:T(8,128)} %param.8) | copy-start | bytes 1572868
  0.7 16.1 %copy-start.1 = (f32[4,4,8,1024]{3,2,1,0:T(8,128)S(1)}, f32[4,4,8,1024]{3,2,1,0:T(8,128)}, u32[]{:S(2)}) copy-start(f32[4,4,8,1024]{3,2,1,0:T(8,128)} %param.7) | copy-start | bytes 1572868
